TPU v7x, 32 devices: a whole 2x2x4 slice. The times are simulated.
32 devices in a mesh: grp: 2 (over x), row: 16 (over z, y, core).
Axes of the slice: x: 2, y: 2, z: 4, core: 2. Of those that a mesh axis runs over, the one named last changes fastest.
Arguments:
- stacked_homolog_states: bfloat16 [128, 256, 256], P('grp', 'row'), parts along dimension 0, may hold values from -6 to 6
- pairwise_activations: bfloat16 [512, 256, 128], P(('grp', 'row')), parts along dimension 0, may hold values from -6 to 6
- normalizer_factor: float32 [256], replicated, may hold values from 0.1 to 1.9
- normalizer_shift: float32 [256], replicated, may hold values from -3 to 3
- former_linear_matrix: bfloat16 [256, 32], replicated, may hold values from -0.375 to 0.375
- left_projection_bias: float32 [32], replicated, may hold values from -3 to 3
- latter_linear_matrix: bfloat16 [256, 32], replicated, may hold values from -0.375 to 0.375
- right_projection_bias: float32 [32], replicated, may hold values from -3 to 3
- output_projection_weight: bfloat16 [1024, 128], replicated, may hold values from -0.75 to 0.75
- output_bias_vector: float32 [128], replicated, may hold values from -3 to 3
Outputs:
- pair_rows: bfloat16 [512, 256, 128], P(('grp', 'row')), parts along dimension 0
- pair_cols: bfloat16 [512, 256, 128], P(('grp', 'row')), parts along dimension 0
There are 2 independent parts, one for each index of `grp`. A program takes and returns all parts, laid end to end along the dimension named above; an argument that names none is the same for every part. Nothing has to cross between parts.
All inputs are finite; a program needn't handle non-finite values.
Results may differ from a plain program's by a relative error of at most 0.0053.
Values may be sent and summed in bfloat16 or wider, within the bound.
No kernel may reach another device: no remote copies, remote signals or barrier semaphores. Data moves between devices by JAX's collectives and lax.ppermute only.
A program may use at most 128 MiB of HBM per device.

v0:
```python
import math

import jax
import jax.numpy as jnp
from jax import lax
from jax.sharding import PartitionSpec as P


def project_alignment(
    stacked_homolog_states,
    normalizer_factor,
    normalizer_shift,
    former_linear_matrix,
    left_projection_bias,
    latter_linear_matrix,
    right_projection_bias,
):
    outer_value_grid = stacked_homolog_states.astype(jnp.float32)
    center = jnp.mean(outer_value_grid, axis=-1, keepdims=True)
    spread = jnp.mean((outer_value_grid - center) ** 2, axis=-1, keepdims=True)
    normed = (
        (outer_value_grid - center) * lax.rsqrt(spread + 1e-05) * normalizer_factor
        + normalizer_shift
    ).astype(jnp.bfloat16)
    left_activations = (
        jnp.dot(normed, former_linear_matrix, preferred_element_type=jnp.float32)
        + left_projection_bias
    ).astype(jnp.bfloat16)
    right_activations = (
        jnp.dot(normed, latter_linear_matrix, preferred_element_type=jnp.float32)
        + right_projection_bias
    ).astype(jnp.bfloat16)
    return (left_activations, right_activations)


def make_panel(local_proj, pair_local, output_projection_weight, output_bias_vector):
    seq_count = local_proj.shape[0]
    own_rows = local_proj.shape[1]
    inner = output_projection_weight.shape[0]
    pair_width = output_projection_weight.shape[1]

    def panel(panel_piece, panel_start):
        panel_len = panel_piece.shape[1]
        block_len = math.gcd(panel_len, 128)

        def one_block(block_id):
            offset = block_id * block_len
            columns = lax.dynamic_slice_in_dim(panel_piece, offset, block_len, 1)
            pair_slice = lax.dynamic_slice_in_dim(pair_local, offset, block_len, 1)
            outer = jnp.einsum(
                "sic,sjd->ijcd", local_proj, columns, preferred_element_type=jnp.float32
            )
            outer = (outer * (1.0 / seq_count)).astype(jnp.bfloat16)
            flat = outer.reshape(own_rows * block_len, inner)
            update = (
                jnp.dot(flat, output_projection_weight, preferred_element_type=jnp.float32)
                + output_bias_vector
            )
            return (pair_slice + update.reshape(own_rows, block_len, pair_width)).astype(
                jnp.bfloat16
            )

        blocks_out = lax.map(one_block, jnp.arange(panel_len // block_len, dtype=jnp.int32))
        return jnp.swapaxes(blocks_out, 0, 1).reshape(own_rows, panel_len, pair_width)

    return panel


def body(
    stacked_homolog_states,
    pairwise_activations,
    normalizer_factor,
    normalizer_shift,
    former_linear_matrix,
    left_projection_bias,
    latter_linear_matrix,
    right_projection_bias,
    output_projection_weight,
    output_bias_vector,
):
    left_activations, right_activations = project_alignment(
        stacked_homolog_states,
        normalizer_factor,
        normalizer_shift,
        former_linear_matrix,
        left_projection_bias,
        latter_linear_matrix,
        right_projection_bias,
    )
    row_panel = make_panel(
        left_activations, pairwise_activations, output_projection_weight, output_bias_vector
    )
    pair_rows = row_panel(
        lax.all_gather(right_activations, "row", axis=1, tiled=True), jnp.int32(0)
    )
    swapped = lax.all_to_all(pair_rows, "row", split_axis=1, concat_axis=0, tiled=True)
    pair_cols = jnp.swapaxes(swapped, 0, 1)
    return (pair_rows, pair_cols)


def solution(mesh):
    in_specs = (
        P("grp", "row", None),
        P(("grp", "row"), None, None),
        P(),
        P(),
        P(),
        P(),
        P(),
        P(),
        P(),
        P(),
    )
    out_specs = (P(("grp", "row"), None, None), P(("grp", "row"), None, None))
    return jax.shard_map(body, mesh=mesh, in_specs=in_specs, out_specs=out_specs, check_vma=False)
```

profile of v0, /device:TPU:0, one launch (start us, length us, event | category | flops | bytes accessed | tf_op | source)
XLA Modules:
  0.0 123.2 jit_solution(7386510076073090636)
XLA Ops:
  7.2 0.0 copy-start
  7.2 0.0 all-gather.2.cloned.1.call-start
  7.2 1.3 %convert_reduce_fusion = f32[64,16]{1,0:T(8,128)S(1)} fusion(bf16[64,16,256]{2,1,0:T(8,128)(2,1)} %param.12), kind=kLoop, calls=%fused_computation.14 | loop fusion | flops 523264 | bytes 528384 | tf_op jit(solution)/shard_map/reduce_sum | solution.py:19
  8.5 1.4 %fusion.17 = f32[64,16]{1,0:T(8,128)S(1)} fusion(bf16[64,16,256]{2,1,0:T(8,128)(2,1)} %param.12, f32[64,16]{1,0:T(8,128)S(1)} %broadcast_multiply_fusion), kind=kLoop, calls=%fused_computation.21 | loop fusion | flops 1047552 | bytes 532480 | tf_op jit(solution)/shard_map/reduce_sum | solution.py:20
  9.9 0.0 copy-done
  9.9 2.2 %fusion.15 = bf16[64,16,32]{2,1,0:T(8,128)(2,1)} fusion(f32[32]{0:T(128)} %param.19, bf16[64,16,256]{2,1,0:T(8,128)(2,1)} %param.12, f32[256]{0:T(256)} %param.15, f32[256]{0:T(256)} %param.14, f32[64,16]{1,0:T(8,128)S(1)} %add_rsqrt_fusion, f32[64,16]{1,0:T(8,128)S(1)} %broadcast_multiply_fusion, bf16[256,32]{0,1:T(8,128)(2,1)S(1)} %copy-done), kind=kOutput, calls=%fused_computation.19 | convolution fusion | flops 18415616 | bytes 616576 | tf_op jit(solution)/shard_map/dot_general | solution.py:30
  12.2 0.0 copy-start.1
  12.2 0.0 copy-start.2
  12.2 0.0 all-gather.2.cloned.1.call-update
  12.2 1.6 %fusion.16 = bf16[64,16,32]{2,1,0:T(8,128)(2,1)S(1)} fusion(f32[32]{0:T(128)} %param.17, bf16[64,16,256]{2,1,0:T(8,128)(2,1)} %param.12, f32[256]{0:T(256)} %param.15, f32[256]{0:T(256)} %param.14, f32[64,16]{1,0:T(8,128)S(1)} %add_rsqrt_fusion, f32[64,16]{1,0:T(8,128)S(1)} %broadcast_multiply_fusion, bf16[256,32]{0,1:T(8,128)(2,1)} %param.16), kind=kOutput, calls=%fused_computation.20 | convolution fusion | flops 18415616 | bytes 616576 | tf_op jit(solution)/shard_map/dot_general | solution.py:26
  13.9 0.3 copy.23
  14.1 54.1 %all-gather.2.cloned.1.call-done = bf16[64,256,32]{2,1,0:T(8,128)(2,1)} async-done(((bf16[64,16,32]{2,1,0:T(8,128)(2,1)}), bf16[64,256,32]{2,1,0:T(8,128)(2,1)}) %all-gather.2.cloned.1.call-update) | async-done | bytes 1048592 | tf_op jit(solution)/shard_map/all_gather | solution.py:94
  68.3 3.9 %copy.22 = bf16[64,256,32]{1,0,2:T(8,128)(2,1)S(1)} copy(bf16[64,256,32]{2,1,0:T(8,128)(2,1)} %all-gather.2.cloned.1.call-done) | data formatting | bytes 2097152 | tf_op jit(solution)/shard_map/while | solution.py:63
  72.2 0.5 iota.3
  72.7 0.0 copy-done.1
  72.7 0.0 copy-done.2
  72.7 14.2 %while.10 = (s32[]{:T(128)}, bf16[2,16,128,128]{3,2,1,0:T(8,128)(2,1)S(1)}, s32[2]{0:T(128)}, bf16[16,256,128]{2,1,0:T(8,128)(2,1)S(1)}, bf16[64,256,32]{1,0,2:T...) while((s32[]{:T(128)}, ...), condition=%wide.region_3.4_spmd, body=%wide.region_2.3_spmd.sunk | while | flops 810549248 | bytes 20843224 | solution.py:63
  72.7 1.2 %dynamic_slice.20 = s32[1]{0:T(128)} dynamic-slice(s32[2]{0:T(128)} %get-tuple-element.162, s32[]{:T(128)} %get-tuple-element.148), dynamic_slice_sizes={1} | dynamic-slice | bytes 12 | tf_op jit(solution)/shard_map/while/body/jit(dynamic_index_in_dim)/dynamic_slice | solution.py:63
  74.6 1.2 fusion.37
  75.8 0.0 copy-start.3
  75.8 1.6 %copy.38 = bf16[16,128,32,32]{1,0,3,2:T(8,128)(2,1)S(1)} copy(bf16[16,128,32,32]{1,2,0,3:T(8,128)(2,1)S(1)} %fusion.37) | data formatting | bytes 8388608 | tf_op jit(solution)/shard_map/while/body/eval_jaxpr/convert_element_type | solution.py:53
  77.4 0.0 copy-done.3
  77.5 2.1 %fusion.38 = f32[2048,128]{1,0:T(8,128)S(1)} fusion(bf16[1024,128]{1,0:T(8,128)(2,1)S(1)} %get-tuple-element.166, bf16[128,8,16,128]{3,2,1,0:T(8,128)(2,1)S(1)} %bitcast.58, f32[128]{0:T(128)S(1)} %copy-done.3), kind=kOutput, calls=%fused_computation.5.clone.1 | convolution fusion | flops 537133056 | bytes 5505536 | tf_op jit(solution)/shard_map/while/body/eval_jaxpr/dot_general | solution.py:56
  79.6 0.2 fusion.39
  79.8 1.3 %dynamic_slice.20 = s32[1]{0:T(128)} dynamic-slice(s32[2]{0:T(128)} %get-tuple-element.162, s32[]{:T(128)} %get-tuple-element.148), dynamic_slice_sizes={1} | dynamic-slice | bytes 12 | tf_op jit(solution)/shard_map/while/body/jit(dynamic_index_in_dim)/dynamic_slice | solution.py:63
  81.7 1.2 fusion.37
  82.9 0.0 copy-start.3
  82.9 1.6 %copy.38 = bf16[16,128,32,32]{1,0,3,2:T(8,128)(2,1)S(1)} copy(bf16[16,128,32,32]{1,2,0,3:T(8,128)(2,1)S(1)} %fusion.37) | data formatting | bytes 8388608 | tf_op jit(solution)/shard_map/while/body/eval_jaxpr/convert_element_type | solution.py:53
  84.6 0.0 copy-done.3
  84.6 2.1 %fusion.38 = f32[2048,128]{1,0:T(8,128)S(1)} fusion(bf16[1024,128]{1,0:T(8,128)(2,1)S(1)} %get-tuple-element.166, bf16[128,8,16,128]{3,2,1,0:T(8,128)(2,1)S(1)} %bitcast.58, f32[128]{0:T(128)S(1)} %copy-done.3), kind=kOutput, calls=%fused_computation.5.clone.1 | convolution fusion | flops 537133056 | bytes 5505536 | tf_op jit(solution)/shard_map/while/body/eval_jaxpr/dot_general | solution.py:56
  86.7 0.2 fusion.39
  86.9 1.6 %copy.24 = bf16[16,2,128,128]{3,0,2,1:T(8,128)(2,1)} copy(bf16[16,2,128,128]{3,2,0,1:T(8,128)(2,1)S(1)} %bitcast.61) | data formatting | bytes 2097152 | tf_op jit(solution)/shard_map/transpose | solution.py:64
  88.6 3.7 %all-to-all-start = ((bf16[16,256,128]{2,0,1:T(8,128)(2,1)}), bf16[16,256,128]{2,0,1:T(8,128)(2,1)S(1)}, u32[]{:S(2)}, u32[]{:S(2)}) async-start(bf16[16,256,128]{2,0,1:T(8,128)(2,1)} %bitcast.10), calls=%async_computation | async-start | bytes 2097152 | tf_op jit(solution)/shard_map/all_to_all | solution.py:96
  92.2 2.5 %copy.26 = bf16[16,256,128]{2,1,0:T(8,128)(2,1)} copy(bf16[16,256,128]{2,0,1:T(8,128)(2,1)} %bitcast.10) | data formatting | bytes 2097152
  94.7 20.4 %all-to-all-done = bf16[16,256,128]{2,0,1:T(8,128)(2,1)S(1)} async-done(((bf16[16,256,128]{2,0,1:T(8,128)(2,1)}), bf16[16,256,128]{2,0,1:T(8,128)(2,1)S(1)}, u32[]{:S(2)}, u32[]{:S(2)}) %all-to-all-start) | async-done | bytes 1048608 | tf_op jit(solution)/shard_map/all_to_all | solution.py:96
  115.1 1.2 %copy.25 = bf16[16,16,16,128]{3,1,0,2:T(8,128)(2,1)} copy(bf16[16,16,16,128]{3,1,2,0:T(8,128)(2,1)S(1)} %bitcast.60) | data formatting | bytes 2097152 | tf_op jit(solution)/shard_map/all_to_all | solution.py:96
  (3 shorter events, 0.0 us)
Async XLA Ops:
  7.2 2.8 %copy-start = (bf16[256,32]{0,1:T(8,128)(2,1)S(1)}, bf16[256,32]{0,1:T(8,128)(2,1)}, u32[]{:S(2)}) copy-start(bf16[256,32]{0,1:T(8,128)(2,1)} %param.18) | copy-start | bytes 49156
  7.2 61.1 %all-gather.2.cloned.1.call-start = ((), (), s32[]{:S(2)}) async-start(), calls=%async_computation.1 | async-start | bytes 4456448 | tf_op jit(solution)/shard_map/all_gather | solution.py:94
  12.2 60.5 %copy-start.1 = (bf16[16,256,128]{2,1,0:T(8,128)(2,1)S(1)}, bf16[16,256,128]{2,1,0:T(8,128)(2,1)}, u32[]{:S(2)}) copy-start(bf16[16,256,128]{2,1,0:T(8,128)(2,1)} %param.13) | copy-start | bytes 3145732
  12.2 60.5 %copy-start.2 = (bf16[1024,128]{1,0:T(8,128)(2,1)S(1)}, bf16[1024,128]{1,0:T(8,128)(2,1)}, u32[]{:S(2)}) copy-start(bf16[1024,128]{1,0:T(8,128)(2,1)} %param.20) | copy-start | bytes 786436
  75.8 1.6 %copy-start.3 = (f32[128]{0:T(128)S(1)}, f32[128]{0:T(128)}, u32[]{:S(2)}) copy-start(f32[128]{0:T(128)} %get-tuple-element.167) | copy-start | bytes 1540 | tf_op jit(solution)/shard_map/while
  82.9 1.6 %copy-start.3 = (f32[128]{0:T(128)S(1)}, f32[128]{0:T(128)}, u32[]{:S(2)}) copy-start(f32[128]{0:T(128)} %get-tuple-element.167) | copy-start | bytes 1540 | tf_op jit(solution)/shard_map/while
  88.6 26.6 %all-to-all-start = ((bf16[16,256,128]{2,0,1:T(8,128)(2,1)}), bf16[16,256,128]{2,0,1:T(8,128)(2,1)S(1)}, u32[]{:S(2)}, u32[]{:S(2)}) async-start(bf16[16,256,128]{2,0,1:T(8,128)(2,1)} %bitcast.10), calls=%async_computation | async-start | bytes 2097152 | tf_op jit(solution)/shard_map/all_to_all | solution.py:96
Sparse Core Ops, SparseCore 0:
  12.3 55.9 all-gather.1
where the time goes:
time: 125 us; the launch traced here: 123 us
  waiting for transfers between devices  74.6 us (60%)
  local copies, waits for them, and re-layouts  15.8 us (13%)
  between operations  14.1 us (11%)
  matrix products  10.6 us (8%)
  starting transfers between devices  3.69 us (3%)
  other arithmetic  3.05 us (2%)
  loops' own time  1.36 us (1%)
    all_gather x1, waiting for transfers between devices, body(): lax.all_gather(right_activations, 'row', axis=1, tiled=True)  54.1 us
    all_to_all x1, waiting for transfers between devices, body(): lax.all_to_all(pair_rows, 'row', split_axis=1, concat_axis=0, tiled=True)  20.4 us
    dot_general x2, matrix products, one_block(): jnp.dot(flat, output_projection_weight, preferred_element_type=jnp.float32)  4.25 us
    while x2, local copies, waits for them, and re-layouts, panel(): lax.map(one_block, jnp.arange(panel_len // block_len, dtype=jnp.int32))  4.17 us
    all_to_all x1, starting transfers between devices, body(): lax.all_to_all(pair_rows, 'row', split_axis=1, concat_axis=0, tiled=True)  3.66 us
    convert_element_type x2, local copies, waits for them, and re-layouts, one_block(): outer = (outer * (1.0 / seq_count)).astype(jnp.bfloat16)  3.24 us
    unnamed x7, local copies, waits for them, and re-layouts  2.52 us
  transfers between devices with their start and end apart: 2, of which 2 were waited for; matrix products, arithmetic and copies ran while one was open for 4% of the time, Pallas kernels for 0%

commit v1 on v0

v1 whole, which is shorter than its diff:
```python
import functools

import jax
import jax.numpy as jnp
from jax import lax
from jax.experimental import pallas as pl
from jax.experimental.pallas import tpu as pltpu
from jax.sharding import PartitionSpec as P

LANES = 128
MIB = 1 << 20


def _cost(flops, nbytes):
    return pl.CostEstimate(flops=flops, bytes_accessed=nbytes, transcendentals=0)


def _project_kernel(x_ref, g_ref, b_ref, wt_ref, pb_ref, local_ref, first_ref, second_ref, proj, turned):
    seqs, rows, depth = x_ref.shape
    hidden = wt_ref.shape[0] // 2
    half = hidden // 2
    step = 8
    for s in range(0, seqs, step):
        x = x_ref[s : s + step].astype(jnp.float32).reshape(step * rows, depth)
        center = jnp.mean(x, axis=-1, keepdims=True)
        x = x - center
        spread = jnp.mean(x * x, axis=-1, keepdims=True)
        normed = (x * lax.rsqrt(spread + 1e-05) * g_ref[...] + b_ref[...]).astype(jnp.bfloat16)
        y = lax.dot_general(normed, wt_ref[...], (((1,), (1,)), ((), ())), preferred_element_type=jnp.float32)
        y = (y + pb_ref[...]).astype(jnp.bfloat16).astype(jnp.float32)
        proj[s * rows : (s + step) * rows, :] = jnp.concatenate(
            [y, jnp.zeros((step * rows, LANES - 2 * hidden), jnp.float32)], axis=1
        )
    pair = LANES // seqs
    for i in range(0, rows, pair):
        parts = [proj[pl.ds(i + p, seqs, stride=rows), :] for p in range(pair)]
        for p in range(pair):
            local_ref[i + p] = parts[p][:, : 2 * hidden].astype(jnp.bfloat16)
        t = jnp.concatenate(parts, axis=0).T
        for p in range(pair):
            cols = slice(p * seqs, (p + 1) * seqs)
            for which in range(2):
                base = which * hidden
                z = jnp.concatenate([t[base : base + half, cols], t[base + half : base + hidden, cols]], axis=1)
                turned[which, (i + p) * half : (i + p + 1) * half, :] = z
    for r in range(half):
        first_ref[:, r * LANES : (r + 1) * LANES] = turned[0, pl.ds(r, rows, stride=half), :].astype(jnp.bfloat16)
        second_ref[:, r * LANES : (r + 1) * LANES] = turned[1, pl.ds(r, rows, stride=half), :].astype(jnp.bfloat16)


def project(x, g, b, wt, pb):
    seqs, rows, depth = x.shape
    hidden = wt.shape[0] // 2
    flat = jax.ShapeDtypeStruct((rows, hidden * seqs), jnp.bfloat16)
    return pl.pallas_call(
        _project_kernel,
        out_shape=(jax.ShapeDtypeStruct((rows, seqs, 2 * hidden), jnp.bfloat16), flat, flat),
        scratch_shapes=[
            pltpu.VMEM((seqs * rows, LANES), jnp.float32),
            pltpu.VMEM((2, rows * hidden // 2, LANES), jnp.float32),
        ],
        compiler_params=pltpu.CompilerParams(vmem_limit_bytes=24 * MIB),
        cost_estimate=_cost(4_000_000_000, 2_000_000),
        name="project",
    )(x, g, b, wt, pb)


def _spread_kernel(local_ref, w_ref, t_ref, u_ref, wf):
    rows, seqs, both = local_ref.shape
    hidden = both // 2
    half = hidden // 2
    width = w_ref.shape[1]
    wf[...] = w_ref[...].astype(jnp.float32)
    blank = jnp.zeros((hidden, 2 * width), jnp.float32)
    group = 256 // seqs
    for r in range(half):
        wt = jnp.concatenate([wf[pl.ds(r, hidden, stride=hidden), :], wf[pl.ds(r + half, hidden, stride=hidden), :]], axis=1)
        wu = jnp.concatenate([wf[r * hidden : (r + 1) * hidden, :], wf[(r + half) * hidden : (r + half + 1) * hidden, :]], axis=1)
        wt = jnp.concatenate([wt, blank], axis=0).astype(jnp.bfloat16)
        wu = jnp.concatenate([blank, wu], axis=0).astype(jnp.bfloat16)
        for i in range(0, rows, group):
            a = local_ref[i : i + group].reshape(group * seqs, both)
            for out_ref, w in ((t_ref, wt), (u_ref, wu)):
                y = jnp.dot(a, w, preferred_element_type=jnp.float32).astype(jnp.bfloat16)
                for k in range(group):
                    for h in range(2):
                        out_ref[
                            (i + k) // 2,
                            (2 * r + h) * seqs : (2 * r + h + 1) * seqs,
                            (k % 2) * width : (k % 2 + 1) * width,
                        ] = y[k * seqs : (k + 1) * seqs, h * width : (h + 1) * width]


def spread_weights(local, w):
    rows, seqs, both = local.shape
    hidden = both // 2
    width = w.shape[1]
    out = jax.ShapeDtypeStruct((rows // 2, hidden * seqs, 2 * width), jnp.bfloat16)
    return pl.pallas_call(
        _spread_kernel,
        out_shape=(out, out),
        scratch_shapes=[pltpu.VMEM(w.shape, jnp.float32)],
        compiler_params=pltpu.CompilerParams(vmem_limit_bytes=48 * MIB),
        cost_estimate=_cost(6_000_000_000, 17_000_000),
        name="spread_weights",
    )(local, w)


def _gather_rows(me, order, pieces, whole):
    rows = pieces[0].shape[0]
    for k, piece in zip(order, pieces):
        at = pl.multiple_of((me ^ k) * rows, rows)
        whole[pl.ds(at, rows), :] = piece[...]


def _rows_kernel(order, scale, me_ref, bias_ref, pair_ref, t_ref, *refs):
    pieces, out_ref, whole = refs[: len(order)], refs[-2], refs[-1]

    @pl.when(pl.program_id(0) == 0)
    def _():
        _gather_rows(me_ref[0], order, pieces, whole)

    width = bias_ref.shape[1]
    y = jnp.dot(whole[...], t_ref[0], preferred_element_type=jnp.float32)
    for k in range(2):
        up = y[:, k * width : (k + 1) * width] * scale + bias_ref[...]
        out_ref[k] = (pair_ref[k].astype(jnp.float32) + up).astype(jnp.bfloat16)


def update_rows(me, order, scale, bias, pair, t, pieces):
    rows, span, width = pair.shape
    own, inner = pieces[0].shape
    return pl.pallas_call(
        functools.partial(_rows_kernel, order, scale),
        grid=(rows // 2,),
        in_specs=[
            pl.BlockSpec(memory_space=pltpu.SMEM),
            pl.BlockSpec((1, width), lambda i: (0, 0)),
            pl.BlockSpec((2, span, width), lambda i: (i, 0, 0)),
            pl.BlockSpec((1, inner, 2 * width), lambda i: (i, 0, 0)),
        ]
        + [pl.BlockSpec((own, inner), lambda i: (0, 0))] * len(order),
        out_specs=pl.BlockSpec((2, span, width), lambda i: (i, 0, 0)),
        out_shape=jax.ShapeDtypeStruct(pair.shape, jnp.bfloat16),
        scratch_shapes=[pltpu.VMEM((span, inner), jnp.bfloat16)],
        compiler_params=pltpu.CompilerParams(vmem_limit_bytes=48 * MIB),
        cost_estimate=_cost(3_000_000_000, 12_000_000),
        name="update_rows",
    )(me, bias, pair, t, *pieces)


def _cols_kernel(order, scale, me_ref, bias_ref, got_ref, t_ref, *refs):
    pieces, out_ref, whole, turned = refs[: len(order)], refs[-3], refs[-2], refs[-1]
    count, rows, _, width = got_ref.shape

    @pl.when(pl.program_id(0) == 0)
    def _():
        _gather_rows(me_ref[0], order, pieces, whole)
        n = rows * rows
        a = lax.broadcasted_iota(jnp.int32, (n, n), 0)
        b = lax.broadcasted_iota(jnp.int32, (n, n), 1)
        swap = ((a % rows) * rows + a // rows == b).astype(jnp.bfloat16)
        for c in range(count):
            y = jnp.dot(swap, got_ref[c].reshape(n, width), preferred_element_type=jnp.float32)
            turned[:, c * rows : (c + 1) * rows, :] = y.astype(jnp.bfloat16).reshape(rows, rows, width)

    y = jnp.dot(whole[...], t_ref[0], preferred_element_type=jnp.float32)
    i = pl.program_id(0)
    for k in range(2):
        up = y[:, k * width : (k + 1) * width] * scale + bias_ref[...]
        out_ref[k] = (turned[2 * i + k].astype(jnp.float32) + up).astype(jnp.bfloat16)


def update_cols(me, order, scale, bias, got, t, pieces):
    count, rows, _, width = got.shape
    span = count * rows
    own, inner = pieces[0].shape
    return pl.pallas_call(
        functools.partial(_cols_kernel, order, scale),
        grid=(rows // 2,),
        in_specs=[
            pl.BlockSpec(memory_space=pltpu.SMEM),
            pl.BlockSpec((1, width), lambda i: (0, 0)),
            pl.BlockSpec(got.shape, lambda i: (0, 0, 0, 0)),
            pl.BlockSpec((1, inner, 2 * width), lambda i: (i, 0, 0)),
        ]
        + [pl.BlockSpec((own, inner), lambda i: (0, 0))] * len(order),
        out_specs=pl.BlockSpec((2, span, width), lambda i: (i, 0, 0)),
        out_shape=jax.ShapeDtypeStruct((rows, span, width), jnp.bfloat16),
        scratch_shapes=[pltpu.VMEM((span, inner), jnp.bfloat16), pltpu.VMEM((rows, span, width), jnp.bfloat16)],
        compiler_params=pltpu.CompilerParams(vmem_limit_bytes=56 * MIB),
        cost_estimate=_cost(3_000_000_000, 12_000_000),
        name="update_cols",
    )(me, bias, got, t, *pieces)


def gather_pieces(x, n):
    pieces, order = [x], [0]
    k = n // 2
    while k:
        pairs = [(i, i ^ k) for i in range(n)]
        pieces = pieces + [lax.ppermute(p, "row", pairs) for p in pieces]
        order = order + [o ^ k for o in order]
        k //= 2
    return pieces, tuple(order)


def body(n, x, pair, g, b, w1, b1, w2, b2, w, bias):
    seqs, rows, depth = x.shape
    width = pair.shape[-1]
    me = lax.axis_index("row").astype(jnp.int32).reshape(1)
    wt = jnp.concatenate([w1.T, w2.T], axis=0)
    pb = jnp.concatenate([b1, b2]).reshape(1, -1)
    blocks = pair.reshape(rows, n, rows, width).transpose(1, 0, 2, 3)
    got = lax.all_to_all(blocks, "row", split_axis=0, concat_axis=0, tiled=True)
    local, first, second = project(x, g.reshape(1, depth), b.reshape(1, depth), wt, pb)
    seconds, order = gather_pieces(second, n)
    firsts, _ = gather_pieces(first, n)
    t, u = spread_weights(local, w)
    scale = 1.0 / seqs
    bias = bias.reshape(1, width)
    pair_rows = update_rows(me, order, scale, bias, pair, t, seconds)
    pair_cols = update_cols(me, order, scale, bias, got, u, firsts)
    return pair_rows, pair_cols


def solution(mesh):
    pair_spec = P(("grp", "row"), None, None)
    in_specs = (P("grp", "row", None), pair_spec) + (P(),) * 8
    return jax.shard_map(
        functools.partial(body, mesh.shape["row"]),
        mesh=mesh,
        in_specs=in_specs,
        out_specs=(pair_spec, pair_spec),
        check_vma=False,
    )
```

time: 125 us -> 90.8 us (0.73)
  waiting for transfers between devices: 74.6 us -> 26.3 us
  Pallas kernels: 0 us -> 29.6 us
  starting transfers between devices: 3.69 us -> 25.9 us
  between operations: 14.1 us -> 0.81 us
  matrix products: 10.6 us -> 0 us
  local copies, waits for them, and re-layouts: 15.8 us -> 5.89 us
  other arithmetic: 3.05 us -> 1.49 us
  loops' own time: 1.36 us -> 0 us
    all_gather x1 -> x0, waiting for transfers between devices: 54.1 us -> none  [body(): lax.all_gather(right_activations, 'row', axis=1, tiled=True)]
    pallas_call x0 -> x4, Pallas kernels: none -> 29.6 us  [the longest x1 10.3 us: spread_weights(): pl.pallas_call(_spread_kernel, out_shape=(out, out), scratch_shapes=[pltp...]
    ppermute x0 -> x30, waiting for transfers between devices: none -> 26.3 us  [gather_pieces(): pieces = pieces + [lax.ppermute(p, 'row', pairs) for p in pieces]]
    all_to_all x1, waiting for transfers between devices: 20.4 us -> 0.01 us  [body(): got = lax.all_to_all(blocks, 'row', split_axis=0, concat_axis=0, tiled=True)]
    ppermute x0 -> x30, starting transfers between devices: none -> 18.4 us  [gather_pieces(): pieces = pieces + [lax.ppermute(p, 'row', pairs) for p in pieces]]
    dot_general x6 -> x0, matrix products: 10.6 us -> none  [the longest x2 4.25 us: one_block(): jnp.dot(flat, output_projection_weight, preferred_element_type=jnp.float32)]
    while x6 -> x0, local copies, waits for them, and re-layouts: 4.19 us -> none  [the longest x2 4.17 us: panel(): lax.map(one_block, jnp.arange(panel_len // block_len, dtype=jnp.int32))]
    all_to_all x1, starting transfers between devices: 3.66 us -> 7.52 us  [body(): got = lax.all_to_all(blocks, 'row', split_axis=0, concat_axis=0, tiled=True)]
  transfers between devices with their start and end apart: 2 -> 31, of which waited for: 2 -> 8; matrix products, arithmetic and copies ran while one was open for 4% -> 2% of each run, Pallas kernels for 0% -> 22%
where the time goes in v1:
time: 90.8 us; the launch traced here: 90.1 us
  Pallas kernels  29.6 us (33%)
  waiting for transfers between devices  26.3 us (29%)
  starting transfers between devices  25.9 us (29%)
  local copies, waits for them, and re-layouts  5.89 us (6%)
  other arithmetic  1.49 us (2%)
    ppermute x30, waiting for transfers between devices, gather_pieces(): pieces = pieces + [lax.ppermute(p, 'row', pairs) for p in pieces]  26.3 us
    ppermute x30, starting transfers between devices, gather_pieces(): pieces = pieces + [lax.ppermute(p, 'row', pairs) for p in pieces]  18.4 us
    pallas_call x1, Pallas kernels, spread_weights(): pl.pallas_call(_spread_kernel, out_shape=(out, out), scratch_shapes=[pltp...  10.3 us
    pallas_call x1, Pallas kernels, update_cols(): pl.pallas_call(functools.partial(_cols_kernel, order, scale), grid=(rows...  9.66 us
    pallas_call x1, Pallas kernels, update_rows(): pl.pallas_call(functools.partial(_rows_kernel, order, scale), grid=(rows...  8.44 us
    all_to_all x1, starting transfers between devices, body(): got = lax.all_to_all(blocks, 'row', split_axis=0, concat_axis=0, tiled=True)  7.52 us
    unnamed x32, local copies, waits for them, and re-layouts  3.42 us
    reshape x1, local copies, waits for them, and re-layouts, body(): blocks = pair.reshape(rows, n, rows, width).transpose(1, 0, 2, 3)  2.47 us
  transfers between devices with their start and end apart: 31, of which 8 were waited for; matrix products, arithmetic and copies ran while one was open for 2% of the time, Pallas kernels for 22%

profile of v1, /device:TPU:0, one launch (start us, length us, event | category | flops | bytes accessed | tf_op | source)
XLA Modules:
  0.0 90.1 jit_solution(6868086350934148852)
XLA Ops:
  0.6 2.5 %copy.14 = bf16[16,16,16,128]{3,2,0,1:T(8,128)(2,1)} copy(bf16[16,16,16,128]{3,2,1,0:T(8,128)(2,1)} %bitcast.12) | data formatting | bytes 2097152 | tf_op jit(solution)/shard_map/reshape | solution.py:214
  3.1 7.5 %all-to-all-start = ((bf16[16,16,16,128]{3,2,1,0:T(8,128)(2,1)}), bf16[16,16,16,128]{3,2,1,0:T(8,128)(2,1)S(1)}, u32[]{:S(2)}, u32[]{:S(2)}) async-start(bf16[16,16,16,128]{3,2,1,0:T(8,128)(2,1)} %bitcast.11), calls=%async_computation | async-start | bytes 2097152 | tf_op jit(solution)/shard_map/all_to_all | solution.py:215
  10.6 0.7 maximum_bitcast_fusion.pb_ref
  11.4 0.7 pad_maximum_fusion.wt_ref
  12.1 1.0 %copy-done.3 = bf16[64,16,256]{2,1,0:T(8,128)(2,1)S(1)} copy-done((bf16[64,16,256]{2,1,0:T(8,128)(2,1)S(1)}, bf16[64,16,256]{2,1,0:T(8,128)(2,1)}, u32[]{:S(2)}) %copy-start.3) | copy-done | bytes 524312
  13.2 0.7 copy-done.5
  13.8 0.7 copy-done.6
  14.5 1.2 %project.1 = (bf16[16,64,64]{2,1,0:T(8,128)(2,1)S(1)}, bf16[16,2048]{1,0:T(8,128)(2,1)S(1)}, bf16[16,2048]{1,0:T(8,128)(2,1)S(1)}) custom-call(bf16[64,16,256]{2,1,0:T(8,128)(2,1)S(1)} %copy-done.3, f32[1,256]{1,0:T(1,128)S(1)} %bitcast.15, f32[1,256]{1,0:T(1,128)S(1)} %bitcast.16, bf16[64,256]{1,0:T(8,128)(2,1)S(1)} %pad_maximum_fusion.wt_ref, ...), custom_call_target="tpu_custom_call" | custom-call | flops 4000000000 | bytes 2000000 | tf_op jit(solution)/shard_map/project/pallas_call | solution.py:55
  15.8 2.9 %collective-permute-start = (bf16[16,2048]{1,0:T(8,128)(2,1)S(1)}, bf16[16,2048]{1,0:T(8,128)(2,1)S(1)}, u32[]{:S(2)}, u32[]{:S(2)}) collective-permute-start(bf16[16,2048]{1,0:T(8,128)(2,1)S(1)} %get-tuple-element.9.refs_0_), channel_id=1, source_target_pairs={{0,8},{1,9},{2,10},{3,11},{4,12},{5,13},{6,14},{7,15},{8,0},{9,1},... | collective-permute-start | bytes 196616 | tf_op jit(solution)/shard_map/ppermute | solution.py:202
  18.7 1.5 %collective-permute-start.1 = (bf16[16,2048]{1,0:T(8,128)(2,1)S(1)}, bf16[16,2048]{1,0:T(8,128)(2,1)S(1)}, u32[]{:S(2)}, u32[]{:S(2)}) collective-permute-start(bf16[16,2048]{1,0:T(8,128)(2,1)S(1)} %get-tuple-element.9.refs_0_), channel_id=1, source_target_pairs={{0,4},{1,5},{2,6},{3,7},{4,0},{5,1},{6,2},{7,3},{8,12},{9,13},{10,... | collective-permute-start | bytes 196616 | tf_op jit(solution)/shard_map/ppermute | solution.py:202
  20.1 1.5 %collective-permute-start.3 = (bf16[16,2048]{1,0:T(8,128)(2,1)S(1)}, bf16[16,2048]{1,0:T(8,128)(2,1)S(1)}, u32[]{:S(2)}, u32[]{:S(2)}) collective-permute-start(bf16[16,2048]{1,0:T(8,128)(2,1)S(1)} %get-tuple-element.9.refs_0_), channel_id=1, source_target_pairs={{0,2},{1,3},{2,0},{3,1},{4,6},{5,7},{6,4},{7,5},{8,10},{9,11},{10,... | collective-permute-start | bytes 196616 | tf_op jit(solution)/shard_map/ppermute | solution.py:202
  21.6 0.0 collective-permute-start.7
  21.6 0.6 collective-permute-start.15
  22.2 19.7 %collective-permute-done.refs_1_ = bf16[16,2048]{1,0:T(8,128)(2,1)S(1)} collective-permute-done((bf16[16,2048]{1,0:T(8,128)(2,1)S(1)}, bf16[16,2048]{1,0:T(8,128)(2,1)S(1)}, u32[]{:S(2)}, u32[]{:S(2)}) %collective-permute-start) | collective-permute-done | bytes 65568 | tf_op jit(solution)/shard_map/ppermute | solution.py:202
  41.9 0.0 collective-permute-start.16
  41.9 1.5 %collective-permute-start.18 = (bf16[16,2048]{1,0:T(8,128)(2,1)S(1)}, bf16[16,2048]{1,0:T(8,128)(2,1)}, u32[]{:S(2)}, u32[]{:S(2)}) collective-permute-start(bf16[16,2048]{1,0:T(8,128)(2,1)S(1)} %get-tuple-element.11.refs_0_), channel_id=1, source_target_pairs={{0,2},{1,3},{2,0},{3,1},{4,6},{5,7},{6,4},{7,5},{8,10},{9,11},{10,... | collective-permute-start | bytes 196616 | tf_op jit(solution)/shard_map/ppermute | solution.py:202
  43.4 0.0 collective-permute-start.22
  43.4 0.0 collective-permute-done.7.refs_8_
  43.4 2.1 %collective-permute-start.2 = (bf16[16,2048]{1,0:T(8,128)(2,1)S(1)}, bf16[16,2048]{1,0:T(8,128)(2,1)S(1)}, u32[]{:S(2)}, u32[]{:S(2)}) collective-permute-start(bf16[16,2048]{1,0:T(8,128)(2,1)S(1)} %collective-permute-done.refs_1_), channel_id=1, source_target_pairs={{0,4},{1,5},{2,6},{3,7},{4,0},{5,1},{6,2},{7,3},{8,12},{9,13},{10,... | collective-permute-start | bytes 196616 | tf_op jit(solution)/shard_map/ppermute | solution.py:202
  45.5 0.5 collective-permute-start.4
  46.0 0.1 collective-permute-done.16.refs_2_
  46.1 1.9 %collective-permute-start.5 = (bf16[16,2048]{1,0:T(8,128)(2,1)S(1)}, bf16[16,2048]{1,0:T(8,128)(2,1)S(1)}, u32[]{:S(2)}, u32[]{:S(2)}) collective-permute-start(bf16[16,2048]{1,0:T(8,128)(2,1)S(1)} %collective-permute-done.1.refs_2_), channel_id=1, source_target_pairs={{0,2},{1,3},{2,0},{3,1},{4,6},{5,7},{6,4},{7,5},{8,10},{9,11},{10,... | collective-permute-start | bytes 196616 | tf_op jit(solution)/shard_map/ppermute | solution.py:202
  48.0 0.0 collective-permute-start.8
  48.0 0.0 collective-permute-done.22.refs_8_
  48.0 0.5 collective-permute-start.9
  48.5 0.1 collective-permute-start.11
  48.6 1.7 %collective-permute-done.4.refs_5_ = bf16[16,2048]{1,0:T(8,128)(2,1)S(1)} collective-permute-done((bf16[16,2048]{1,0:T(8,128)(2,1)S(1)}, bf16[16,2048]{1,0:T(8,128)(2,1)S(1)}, u32[]{:S(2)}, u32[]{:S(2)}) %collective-permute-start.4) | collective-permute-done | bytes 65568 | tf_op jit(solution)/shard_map/ppermute | solution.py:202
  50.3 0.1 collective-permute-start.17
  50.4 0.6 collective-permute-done.5.refs_6_
  51.0 1.3 %collective-permute-start.19 = (bf16[16,2048]{1,0:T(8,128)(2,1)S(1)}, bf16[16,2048]{1,0:T(8,128)(2,1)}, u32[]{:S(2)}, u32[]{:S(2)}) collective-permute-start(bf16[16,2048]{1,0:T(8,128)(2,1)S(1)} %collective-permute-done.15.refs_1_), channel_id=1, source_target_pairs={{0,2},{1,3},{2,0},{3,1},{4,6},{5,7},{6,4},{7,5},{8,10},{9,11},{10,... | collective-permute-start | bytes 196616 | tf_op jit(solution)/shard_map/ppermute | solution.py:202
  52.3 0.0 collective-permute-done.8.refs_9_
  52.3 0.8 collective-permute-start.20
  53.1 0.0 collective-permute-done.9.refs_10_
  53.1 0.0 collective-permute-start.23
  53.1 0.0 collective-permute-done.11.refs_12_
  53.1 0.5 collective-permute-start.24
  53.6 1.1 %collective-permute-done.17.refs_3_ = bf16[16,2048]{1,0:T(8,128)(2,1)} collective-permute-done((bf16[16,2048]{1,0:T(8,128)(2,1)S(1)}, bf16[16,2048]{1,0:T(8,128)(2,1)}, u32[]{:S(2)}, u32[]{:S(2)}) %collective-permute-start.17) | collective-permute-done | bytes 65568 | tf_op jit(solution)/shard_map/ppermute | solution.py:202
  54.7 0.3 collective-permute-start.6
  55.0 0.4 collective-permute-done.19.refs_5_
  55.4 1.7 %collective-permute-done.20.refs_6_ = bf16[16,2048]{1,0:T(8,128)(2,1)} collective-permute-done((bf16[16,2048]{1,0:T(8,128)(2,1)S(1)}, bf16[16,2048]{1,0:T(8,128)(2,1)}, u32[]{:S(2)}, u32[]{:S(2)}) %collective-permute-start.20) | collective-permute-done | bytes 65568 | tf_op jit(solution)/shard_map/ppermute | solution.py:202
  57.1 0.0 collective-permute-start.12
  57.1 0.5 collective-permute-start.13
  57.6 0.4 collective-permute-start.21
  57.9 1.0 %collective-permute-done.6.refs_7_ = bf16[16,2048]{1,0:T(8,128)(2,1)S(1)} collective-permute-done((bf16[16,2048]{1,0:T(8,128)(2,1)S(1)}, bf16[16,2048]{1,0:T(8,128)(2,1)S(1)}, u32[]{:S(2)}, u32[]{:S(2)}) %collective-permute-start.6) | collective-permute-done | bytes 65568 | tf_op jit(solution)/shard_map/ppermute | solution.py:202
  59.0 0.0 collective-permute-start.14
  59.0 0.0 copy-start.2
  59.0 10.3 %spread_weights.1 = (bf16[8,2048,256]{2,1,0:T(8,128)(2,1)}, bf16[8,2048,256]{2,1,0:T(8,128)(2,1)}) custom-call(bf16[16,64,64]{2,1,0:T(8,128)(2,1)S(1)} %get-tuple-element.7.local_ref, bf16[1024,128]{1,0:T(8,128)(2,1)S(1)} %copy-done.4), custom_call_target="tpu_custom_call" | custom-call | flops 6000000000 | bytes 17000000 | tf_op jit(solution)/shard_map/spread_weights/pallas_call | solution.py:99
  69.3 0.6 collective-permute-start.26
  69.9 0.1 collective-permute-start.25
  70.0 0.0 collective-permute-done.13.refs_14_
  70.0 0.4 collective-permute-start.27
  70.4 0.1 collective-permute-start.28
  70.5 0.0 collective-permute-done.14.refs_15_
  70.5 0.4 collective-permute-start.29
  70.9 8.4 %update_rows.1 = bf16[16,256,128]{2,1,0:T(8,128)(2,1)} custom-call(s32[1]{0:T(128)} %bitcast.me_ref, f32[1,128]{1,0:T(1,128)S(1)} %bitcast.14, bf16[16,256,128]{2,1,0:T(8,128)(2,1)S(1)} %copy-done, bf16[8,2048,256]{2,1,0:T(8,128)(2,1)} %get-tuple-element.8.t_ref, bf16[16,2048]{1,0:T(8,128)(2,1)S(1)} %get-tuple-element.9.refs_0_, ...), custom_call_target="tpu_custom_call" | custom-call | flops 3000000000 | bytes 12000000 | tf_op jit(solution)/shard_map/update_rows/pallas_call | solution.py:133
  79.4 0.0 collective-permute-done.27.refs_13_
  79.4 0.0 all-to-all-done.got_ref
  79.4 0.5 copy-done.11
  80.0 0.0 copy-done.12
  80.0 0.0 copy-done.13
  80.0 0.0 copy-done.14
  80.0 0.0 copy-done.15
  80.1 0.4 copy-done.7
  80.4 9.7 %update_cols.1 = bf16[16,256,128]{2,1,0:T(8,128)(2,1)} custom-call(s32[1]{0:T(128)} %bitcast.me_ref, f32[1,128]{1,0:T(1,128)} %bitcast.13, bf16[16,16,16,128]{3,2,1,0:T(8,128)(2,1)} %copy-done.7, bf16[8,2048,256]{2,1,0:T(8,128)(2,1)} %get-tuple-element.10.t_ref, bf16[16,2048]{1,0:T(8,128)(2,1)} %copy-done.1, bf16[16,2048]{1,0:T(8,128)(2,1)} %copy-done.8, ...), custom_call_target="tpu_custom_call" | custom-call | flops 3000000000 | bytes 12000000 | tf_op jit(solution)/shard_map/update_cols/pallas_call | solution.py:178
  (37 shorter events, 0.1 us)
Async XLA Ops:
  3.1 55.9 %copy-start.4 = (bf16[1024,128]{1,0:T(8,128)(2,1)S(1)}, bf16[1024,128]{1,0:T(8,128)(2,1)}, u32[]{:S(2)}) copy-start(bf16[1024,128]{1,0:T(8,128)(2,1)} %w_ref.1) | copy-start | bytes 786436
  3.1 76.3 %all-to-all-start = ((bf16[16,16,16,128]{3,2,1,0:T(8,128)(2,1)}), bf16[16,16,16,128]{3,2,1,0:T(8,128)(2,1)S(1)}, u32[]{:S(2)}, u32[]{:S(2)}) async-start(bf16[16,16,16,128]{3,2,1,0:T(8,128)(2,1)} %bitcast.11), calls=%async_computation | async-start | bytes 2097152 | tf_op jit(solution)/shard_map/all_to_all | solution.py:215
  12.1 1.0 %copy-start.3 = (bf16[64,16,256]{2,1,0:T(8,128)(2,1)S(1)}, bf16[64,16,256]{2,1,0:T(8,128)(2,1)}, u32[]{:S(2)}) copy-start(bf16[64,16,256]{2,1,0:T(8,128)(2,1)} %x_ref.1) | copy-start | bytes 1572868
  13.2 0.7 copy-start.5
  13.8 0.7 copy-start.6
  15.8 53.5 %copy-start.1 = (bf16[16,2048]{1,0:T(8,128)(2,1)}, bf16[16,2048]{1,0:T(8,128)(2,1)S(1)}, u32[]{:S(2)}) copy-start(bf16[16,2048]{1,0:T(8,128)(2,1)S(1)} %get-tuple-element.11.refs_0_) | copy-start | bytes 196612
  15.8 26.1 %collective-permute-start = (bf16[16,2048]{1,0:T(8,128)(2,1)S(1)}, bf16[16,2048]{1,0:T(8,128)(2,1)S(1)}, u32[]{:S(2)}, u32[]{:S(2)}) collective-permute-start(bf16[16,2048]{1,0:T(8,128)(2,1)S(1)} %get-tuple-element.9.refs_0_), channel_id=1, source_target_pairs={{0,8},{1,9},{2,10},{3,11},{4,12},{5,13},{6,14},{7,15},{8,0},{9,1},... | collective-permute-start | bytes 196616 | tf_op jit(solution)/shard_map/ppermute | solution.py:202
  18.7 23.2 %collective-permute-start.1 = (bf16[16,2048]{1,0:T(8,128)(2,1)S(1)}, bf16[16,2048]{1,0:T(8,128)(2,1)S(1)}, u32[]{:S(2)}, u32[]{:S(2)}) collective-permute-start(bf16[16,2048]{1,0:T(8,128)(2,1)S(1)} %get-tuple-element.9.refs_0_), channel_id=1, source_target_pairs={{0,4},{1,5},{2,6},{3,7},{4,0},{5,1},{6,2},{7,3},{8,12},{9,13},{10,... | collective-permute-start | bytes 196616 | tf_op jit(solution)/shard_map/ppermute | solution.py:202
  20.1 23.2 %collective-permute-start.3 = (bf16[16,2048]{1,0:T(8,128)(2,1)S(1)}, bf16[16,2048]{1,0:T(8,128)(2,1)S(1)}, u32[]{:S(2)}, u32[]{:S(2)}) collective-permute-start(bf16[16,2048]{1,0:T(8,128)(2,1)S(1)} %get-tuple-element.9.refs_0_), channel_id=1, source_target_pairs={{0,2},{1,3},{2,0},{3,1},{4,6},{5,7},{6,4},{7,5},{8,10},{9,11},{10,... | collective-permute-start | bytes 196616 | tf_op jit(solution)/shard_map/ppermute | solution.py:202
  21.6 21.8 %collective-permute-start.7 = (bf16[16,2048]{1,0:T(8,128)(2,1)S(1)}, bf16[16,2048]{1,0:T(8,128)(2,1)S(1)}, u32[]{:S(2)}, u32[]{:S(2)}) collective-permute-start(bf16[16,2048]{1,0:T(8,128)(2,1)S(1)} %get-tuple-element.9.refs_0_), channel_id=1, source_target_pairs={{0,1},{1,0},{2,3},{3,2},{4,5},{5,4},{6,7},{7,6},{8,9},{9,8},{10,11... | collective-permute-start | bytes 196616 | tf_op jit(solution)/shard_map/ppermute | solution.py:202
  21.6 23.9 %collective-permute-start.15 = (bf16[16,2048]{1,0:T(8,128)(2,1)S(1)}, bf16[16,2048]{1,0:T(8,128)(2,1)S(1)}, u32[]{:S(2)}, u32[]{:S(2)}) collective-permute-start(bf16[16,2048]{1,0:T(8,128)(2,1)S(1)} %get-tuple-element.11.refs_0_), channel_id=1, source_target_pairs={{0,8},{1,9},{2,10},{3,11},{4,12},{5,13},{6,14},{7,15},{8,0},{9,1},... | collective-permute-start | bytes 196616 | tf_op jit(solution)/shard_map/ppermute | solution.py:202
  41.9 4.3 %collective-permute-start.16 = (bf16[16,2048]{1,0:T(8,128)(2,1)S(1)}, bf16[16,2048]{1,0:T(8,128)(2,1)S(1)}, u32[]{:S(2)}, u32[]{:S(2)}) collective-permute-start(bf16[16,2048]{1,0:T(8,128)(2,1)S(1)} %get-tuple-element.11.refs_0_), channel_id=1, source_target_pairs={{0,4},{1,5},{2,6},{3,7},{4,0},{5,1},{6,2},{7,3},{8,12},{9,13},{10,... | collective-permute-start | bytes 196616 | tf_op jit(solution)/shard_map/ppermute | solution.py:202
  41.9 6.2 %collective-permute-start.18 = (bf16[16,2048]{1,0:T(8,128)(2,1)S(1)}, bf16[16,2048]{1,0:T(8,128)(2,1)}, u32[]{:S(2)}, u32[]{:S(2)}) collective-permute-start(bf16[16,2048]{1,0:T(8,128)(2,1)S(1)} %get-tuple-element.11.refs_0_), channel_id=1, source_target_pairs={{0,2},{1,3},{2,0},{3,1},{4,6},{5,7},{6,4},{7,5},{8,10},{9,11},{10,... | collective-permute-start | bytes 196616 | tf_op jit(solution)/shard_map/ppermute | solution.py:202
  43.4 4.7 %collective-permute-start.22 = (bf16[16,2048]{1,0:T(8,128)(2,1)S(1)}, bf16[16,2048]{1,0:T(8,128)(2,1)}, u32[]{:S(2)}, u32[]{:S(2)}) collective-permute-start(bf16[16,2048]{1,0:T(8,128)(2,1)S(1)} %get-tuple-element.11.refs_0_), channel_id=1, source_target_pairs={{0,1},{1,0},{2,3},{3,2},{4,5},{5,4},{6,7},{7,6},{8,9},{9,8},{10,11... | collective-permute-start | bytes 196616 | tf_op jit(solution)/shard_map/ppermute | solution.py:202
  43.4 5.2 %collective-permute-start.2 = (bf16[16,2048]{1,0:T(8,128)(2,1)S(1)}, bf16[16,2048]{1,0:T(8,128)(2,1)S(1)}, u32[]{:S(2)}, u32[]{:S(2)}) collective-permute-start(bf16[16,2048]{1,0:T(8,128)(2,1)S(1)} %collective-permute-done.refs_1_), channel_id=1, source_target_pairs={{0,4},{1,5},{2,6},{3,7},{4,0},{5,1},{6,2},{7,3},{8,12},{9,13},{10,... | collective-permute-start | bytes 196616 | tf_op jit(solution)/shard_map/ppermute | solution.py:202
  45.5 23.8 %copy-start.8 = (bf16[16,2048]{1,0:T(8,128)(2,1)}, bf16[16,2048]{1,0:T(8,128)(2,1)S(1)}, u32[]{:S(2)}) copy-start(bf16[16,2048]{1,0:T(8,128)(2,1)S(1)} %collective-permute-done.15.refs_1_) | copy-start | bytes 196612
  45.5 4.9 %collective-permute-start.4 = (bf16[16,2048]{1,0:T(8,128)(2,1)S(1)}, bf16[16,2048]{1,0:T(8,128)(2,1)S(1)}, u32[]{:S(2)}, u32[]{:S(2)}) collective-permute-start(bf16[16,2048]{1,0:T(8,128)(2,1)S(1)} %collective-permute-done.refs_1_), channel_id=1, source_target_pairs={{0,2},{1,3},{2,0},{3,1},{4,6},{5,7},{6,4},{7,5},{8,10},{9,11},{10,... | collective-permute-start | bytes 196616 | tf_op jit(solution)/shard_map/ppermute | solution.py:202
  46.1 11.8 %copy-start.9 = (bf16[16,2048]{1,0:T(8,128)(2,1)}, bf16[16,2048]{1,0:T(8,128)(2,1)S(1)}, u32[]{:S(2)}) copy-start(bf16[16,2048]{1,0:T(8,128)(2,1)S(1)} %collective-permute-done.16.refs_2_) | copy-start | bytes 196612
  46.1 4.9 %collective-permute-start.5 = (bf16[16,2048]{1,0:T(8,128)(2,1)S(1)}, bf16[16,2048]{1,0:T(8,128)(2,1)S(1)}, u32[]{:S(2)}, u32[]{:S(2)}) collective-permute-start(bf16[16,2048]{1,0:T(8,128)(2,1)S(1)} %collective-permute-done.1.refs_2_), channel_id=1, source_target_pairs={{0,2},{1,3},{2,0},{3,1},{4,6},{5,7},{6,4},{7,5},{8,10},{9,11},{10,... | collective-permute-start | bytes 196616 | tf_op jit(solution)/shard_map/ppermute | solution.py:202
  48.0 4.3 %collective-permute-start.8 = (bf16[16,2048]{1,0:T(8,128)(2,1)S(1)}, bf16[16,2048]{1,0:T(8,128)(2,1)S(1)}, u32[]{:S(2)}, u32[]{:S(2)}) collective-permute-start(bf16[16,2048]{1,0:T(8,128)(2,1)S(1)} %collective-permute-done.refs_1_), channel_id=1, source_target_pairs={{0,1},{1,0},{2,3},{3,2},{4,5},{5,4},{6,7},{7,6},{8,9},{9,8},{10,11... | collective-permute-start | bytes 196616 | tf_op jit(solution)/shard_map/ppermute | solution.py:202
  48.0 5.0 %collective-permute-start.9 = (bf16[16,2048]{1,0:T(8,128)(2,1)S(1)}, bf16[16,2048]{1,0:T(8,128)(2,1)S(1)}, u32[]{:S(2)}, u32[]{:S(2)}) collective-permute-start(bf16[16,2048]{1,0:T(8,128)(2,1)S(1)} %collective-permute-done.1.refs_2_), channel_id=1, source_target_pairs={{0,1},{1,0},{2,3},{3,2},{4,5},{5,4},{6,7},{7,6},{8,9},{9,8},{10,11... | collective-permute-start | bytes 196616 | tf_op jit(solution)/shard_map/ppermute | solution.py:202
  48.5 4.5 %collective-permute-start.11 = (bf16[16,2048]{1,0:T(8,128)(2,1)S(1)}, bf16[16,2048]{1,0:T(8,128)(2,1)S(1)}, u32[]{:S(2)}, u32[]{:S(2)}) collective-permute-start(bf16[16,2048]{1,0:T(8,128)(2,1)S(1)} %collective-permute-done.3.refs_4_), channel_id=1, source_target_pairs={{0,1},{1,0},{2,3},{3,2},{4,5},{5,4},{6,7},{7,6},{8,9},{9,8},{10,11... | collective-permute-start | bytes 196616 | tf_op jit(solution)/shard_map/ppermute | solution.py:202
  50.3 4.4 %collective-permute-start.17 = (bf16[16,2048]{1,0:T(8,128)(2,1)S(1)}, bf16[16,2048]{1,0:T(8,128)(2,1)}, u32[]{:S(2)}, u32[]{:S(2)}) collective-permute-start(bf16[16,2048]{1,0:T(8,128)(2,1)S(1)} %collective-permute-done.15.refs_1_), channel_id=1, source_target_pairs={{0,4},{1,5},{2,6},{3,7},{4,0},{5,1},{6,2},{7,3},{8,12},{9,13},{10,... | collective-permute-start | bytes 196616 | tf_op jit(solution)/shard_map/ppermute | solution.py:202
  51.0 4.4 %collective-permute-start.19 = (bf16[16,2048]{1,0:T(8,128)(2,1)S(1)}, bf16[16,2048]{1,0:T(8,128)(2,1)}, u32[]{:S(2)}, u32[]{:S(2)}) collective-permute-start(bf16[16,2048]{1,0:T(8,128)(2,1)S(1)} %collective-permute-done.15.refs_1_), channel_id=1, source_target_pairs={{0,2},{1,3},{2,0},{3,1},{4,6},{5,7},{6,4},{7,5},{8,10},{9,11},{10,... | collective-permute-start | bytes 196616 | tf_op jit(solution)/shard_map/ppermute | solution.py:202
  52.3 4.8 %collective-permute-start.20 = (bf16[16,2048]{1,0:T(8,128)(2,1)S(1)}, bf16[16,2048]{1,0:T(8,128)(2,1)}, u32[]{:S(2)}, u32[]{:S(2)}) collective-permute-start(bf16[16,2048]{1,0:T(8,128)(2,1)S(1)} %collective-permute-done.16.refs_2_), channel_id=1, source_target_pairs={{0,2},{1,3},{2,0},{3,1},{4,6},{5,7},{6,4},{7,5},{8,10},{9,11},{10,... | collective-permute-start | bytes 196616 | tf_op jit(solution)/shard_map/ppermute | solution.py:202
  53.1 4.0 %collective-permute-start.23 = (bf16[16,2048]{1,0:T(8,128)(2,1)S(1)}, bf16[16,2048]{1,0:T(8,128)(2,1)}, u32[]{:S(2)}, u32[]{:S(2)}) collective-permute-start(bf16[16,2048]{1,0:T(8,128)(2,1)S(1)} %collective-permute-done.15.refs_1_), channel_id=1, source_target_pairs={{0,1},{1,0},{2,3},{3,2},{4,5},{5,4},{6,7},{7,6},{8,9},{9,8},{10,11... | collective-permute-start | bytes 196616 | tf_op jit(solution)/shard_map/ppermute | solution.py:202
  53.1 4.5 %collective-permute-start.24 = (bf16[16,2048]{1,0:T(8,128)(2,1)S(1)}, bf16[16,2048]{1,0:T(8,128)(2,1)S(1)}, u32[]{:S(2)}, u32[]{:S(2)}) collective-permute-start(bf16[16,2048]{1,0:T(8,128)(2,1)S(1)} %collective-permute-done.16.refs_2_), channel_id=1, source_target_pairs={{0,1},{1,0},{2,3},{3,2},{4,5},{5,4},{6,7},{7,6},{8,9},{9,8},{10,11... | collective-permute-start | bytes 196616 | tf_op jit(solution)/shard_map/ppermute | solution.py:202
  54.7 4.3 %collective-permute-start.6 = (bf16[16,2048]{1,0:T(8,128)(2,1)S(1)}, bf16[16,2048]{1,0:T(8,128)(2,1)S(1)}, u32[]{:S(2)}, u32[]{:S(2)}) collective-permute-start(bf16[16,2048]{1,0:T(8,128)(2,1)S(1)} %collective-permute-done.2.refs_3_), channel_id=1, source_target_pairs={{0,2},{1,3},{2,0},{3,1},{4,6},{5,7},{6,4},{7,5},{8,10},{9,11},{10,... | collective-permute-start | bytes 196616 | tf_op jit(solution)/shard_map/ppermute | solution.py:202
  55.4 13.9 %collective-permute-start.10 = (bf16[16,2048]{1,0:T(8,128)(2,1)S(1)}, bf16[16,2048]{1,0:T(8,128)(2,1)S(1)}, u32[]{:S(2)}, u32[]{:S(2)}) collective-permute-start(bf16[16,2048]{1,0:T(8,128)(2,1)S(1)} %collective-permute-done.2.refs_3_), channel_id=1, source_target_pairs={{0,1},{1,0},{2,3},{3,2},{4,5},{5,4},{6,7},{7,6},{8,9},{9,8},{10,11... | collective-permute-start | bytes 196616 | tf_op jit(solution)/shard_map/ppermute | solution.py:202
  57.1 12.8 %collective-permute-start.12 = (bf16[16,2048]{1,0:T(8,128)(2,1)S(1)}, bf16[16,2048]{1,0:T(8,128)(2,1)S(1)}, u32[]{:S(2)}, u32[]{:S(2)}) collective-permute-start(bf16[16,2048]{1,0:T(8,128)(2,1)S(1)} %collective-permute-done.4.refs_5_), channel_id=1, source_target_pairs={{0,1},{1,0},{2,3},{3,2},{4,5},{5,4},{6,7},{7,6},{8,9},{9,8},{10,11... | collective-permute-start | bytes 196616 | tf_op jit(solution)/shard_map/ppermute | solution.py:202
  57.1 12.9 %collective-permute-start.13 = (bf16[16,2048]{1,0:T(8,128)(2,1)S(1)}, bf16[16,2048]{1,0:T(8,128)(2,1)S(1)}, u32[]{:S(2)}, u32[]{:S(2)}) collective-permute-start(bf16[16,2048]{1,0:T(8,128)(2,1)S(1)} %collective-permute-done.5.refs_6_), channel_id=1, source_target_pairs={{0,1},{1,0},{2,3},{3,2},{4,5},{5,4},{6,7},{7,6},{8,9},{9,8},{10,11... | collective-permute-start | bytes 196616 | tf_op jit(solution)/shard_map/ppermute | solution.py:202
  57.6 11.7 %copy-start.10 = (bf16[16,2048]{1,0:T(8,128)(2,1)}, bf16[16,2048]{1,0:T(8,128)(2,1)S(1)}, u32[]{:S(2)}) copy-start(bf16[16,2048]{1,0:T(8,128)(2,1)S(1)} %collective-permute-done.24.refs_10_) | copy-start | bytes 196612
  57.6 12.8 %collective-permute-start.21 = (bf16[16,2048]{1,0:T(8,128)(2,1)}, bf16[16,2048]{1,0:T(8,128)(2,1)}, u32[]{:S(2)}, u32[]{:S(2)}) collective-permute-start(bf16[16,2048]{1,0:T(8,128)(2,1)} %collective-permute-done.17.refs_3_), channel_id=1, source_target_pairs={{0,2},{1,3},{2,0},{3,1},{4,6},{5,7},{6,4},{7,5},{8,10},{9,11},{10,... | collective-permute-start | bytes 196616 | tf_op jit(solution)/shard_map/ppermute | solution.py:202
  59.0 11.5 %collective-permute-start.14 = (bf16[16,2048]{1,0:T(8,128)(2,1)S(1)}, bf16[16,2048]{1,0:T(8,128)(2,1)S(1)}, u32[]{:S(2)}, u32[]{:S(2)}) collective-permute-start(bf16[16,2048]{1,0:T(8,128)(2,1)S(1)} %collective-permute-done.6.refs_7_), channel_id=1, source_target_pairs={{0,1},{1,0},{2,3},{3,2},{4,5},{5,4},{6,7},{7,6},{8,9},{9,8},{10,11... | collective-permute-start | bytes 196616 | tf_op jit(solution)/shard_map/ppermute | solution.py:202
  59.0 11.9 %copy-start = (bf16[16,256,128]{2,1,0:T(8,128)(2,1)S(1)}, bf16[16,256,128]{2,1,0:T(8,128)(2,1)}, u32[]{:S(2)}) copy-start(bf16[16,256,128]{2,1,0:T(8,128)(2,1)} %pair_ref.1) | copy-start | bytes 3145732
  59.0 11.9 %copy-start.2 = (f32[128]{0:T(128)S(1)}, f32[128]{0:T(128)}, u32[]{:S(2)}) copy-start(f32[128]{0:T(128)} %param.19) | copy-start | bytes 1540
  69.3 10.0 %collective-permute-start.26 = (bf16[16,2048]{1,0:T(8,128)(2,1)}, bf16[16,2048]{1,0:T(8,128)(2,1)S(1)}, u32[]{:S(2)}, u32[]{:S(2)}) collective-permute-start(bf16[16,2048]{1,0:T(8,128)(2,1)} %collective-permute-done.18.refs_4_), channel_id=1, source_target_pairs={{0,1},{1,0},{2,3},{3,2},{4,5},{5,4},{6,7},{7,6},{8,9},{9,8},{10,11... | collective-permute-start | bytes 196616 | tf_op jit(solution)/shard_map/ppermute | solution.py:202
  69.9 9.5 %collective-permute-start.25 = (bf16[16,2048]{1,0:T(8,128)(2,1)}, bf16[16,2048]{1,0:T(8,128)(2,1)S(1)}, u32[]{:S(2)}, u32[]{:S(2)}) collective-permute-start(bf16[16,2048]{1,0:T(8,128)(2,1)} %collective-permute-done.17.refs_3_), channel_id=1, source_target_pairs={{0,1},{1,0},{2,3},{3,2},{4,5},{5,4},{6,7},{7,6},{8,9},{9,8},{10,11... | collective-permute-start | bytes 196616 | tf_op jit(solution)/shard_map/ppermute | solution.py:202
  70.0 9.4 %collective-permute-start.27 = (bf16[16,2048]{1,0:T(8,128)(2,1)}, bf16[16,2048]{1,0:T(8,128)(2,1)S(1)}, u32[]{:S(2)}, u32[]{:S(2)}) collective-permute-start(bf16[16,2048]{1,0:T(8,128)(2,1)} %collective-permute-done.19.refs_5_), channel_id=1, source_target_pairs={{0,1},{1,0},{2,3},{3,2},{4,5},{5,4},{6,7},{7,6},{8,9},{9,8},{10,11... | collective-permute-start | bytes 196616 | tf_op jit(solution)/shard_map/ppermute | solution.py:202
  70.4 9.0 %collective-permute-start.28 = (bf16[16,2048]{1,0:T(8,128)(2,1)}, bf16[16,2048]{1,0:T(8,128)(2,1)S(1)}, u32[]{:S(2)}, u32[]{:S(2)}) collective-permute-start(bf16[16,2048]{1,0:T(8,128)(2,1)} %collective-permute-done.20.refs_6_), channel_id=1, source_target_pairs={{0,1},{1,0},{2,3},{3,2},{4,5},{5,4},{6,7},{7,6},{8,9},{9,8},{10,11... | collective-permute-start | bytes 196616 | tf_op jit(solution)/shard_map/ppermute | solution.py:202
  70.5 8.9 %collective-permute-start.29 = (bf16[16,2048]{1,0:T(8,128)(2,1)}, bf16[16,2048]{1,0:T(8,128)(2,1)S(1)}, u32[]{:S(2)}, u32[]{:S(2)}) collective-permute-start(bf16[16,2048]{1,0:T(8,128)(2,1)} %collective-permute-done.21.refs_7_), channel_id=1, source_target_pairs={{0,1},{1,0},{2,3},{3,2},{4,5},{5,4},{6,7},{7,6},{8,9},{9,8},{10,11... | collective-permute-start | bytes 196616 | tf_op jit(solution)/shard_map/ppermute | solution.py:202
  79.3 0.6 copy-start.11
  79.4 0.7 copy-start.12
  79.4 0.6 copy-start.13
  79.4 0.6 copy-start.14
  79.4 0.6 copy-start.15
  79.4 1.0 %copy-start.7 = (bf16[16,16,16,128]{3,2,1,0:T(8,128)(2,1)}, bf16[16,16,16,128]{3,2,1,0:T(8,128)(2,1)S(1)}, u32[]{:S(2)}) copy-start(bf16[16,16,16,128]{3,2,1,0:T(8,128)(2,1)S(1)} %all-to-all-done.got_ref) | copy-start | bytes 3145732

commit v2 on v1

v2 whole, which is shorter than its diff:
```python
import functools

import jax
import jax.numpy as jnp
from jax import lax
from jax.experimental import pallas as pl
from jax.experimental.pallas import tpu as pltpu
from jax.sharding import PartitionSpec as P

LANES = 128
MIB = 1 << 20
ANY = pl.BlockSpec(memory_space=pl.ANY)
VMEM = pl.BlockSpec(memory_space=pltpu.VMEM)
SMEM = pl.BlockSpec(memory_space=pltpu.SMEM)


def _cost(flops, nbytes):
    return pl.CostEstimate(flops=flops, bytes_accessed=nbytes, transcendentals=0)


def _project_kernel(
    n, x_hbm, pair_hbm, g_hbm, b_hbm, w1_hbm, c1_hbm, w2_hbm, c2_hbm, w_hbm, local_ref, flat_ref, out_w_ref, mine_ref, theirs_ref, *refs
):
    x_ref, pair_ref, g_ref, b_ref, w_ref, c_ref, proj, turned, in_sem, x_sem, sem = refs
    me = lax.axis_index("row")
    seqs, rows, depth = x_ref.shape
    hidden = w_ref.shape[0] // 2
    half = hidden // 2
    step = 8
    loads = [
        pltpu.make_async_copy(src, dst, in_sem.at[k])
        for k, (src, dst) in enumerate(
            (
                (g_hbm, g_ref),
                (b_hbm, b_ref),
                (w1_hbm, w_ref.at[pl.ds(0, hidden), :]),
                (w2_hbm, w_ref.at[pl.ds(hidden, hidden), :]),
                (c1_hbm, c_ref.at[0]),
                (c2_hbm, c_ref.at[1]),
            )
        )
    ]
    part = seqs // 2
    chunks = [
        pltpu.make_async_copy(x_hbm.at[pl.ds(k * part, part)], x_ref.at[pl.ds(k * part, part)], x_sem.at[k])
        for k in range(2)
    ]
    others = [pltpu.make_async_copy(pair_hbm, pair_ref, sem.at[0]), pltpu.make_async_copy(w_hbm, out_w_ref, sem.at[1])]
    for c in chunks[:1] + loads + chunks[1:] + others:
        c.start()
    for c in loads:
        c.wait()
    bias = jnp.concatenate([c_ref[0], c_ref[1]], axis=1)
    for s in range(0, seqs, step):
        if s % part == 0:
            chunks[s // part].wait()
        x = x_ref[s : s + step].astype(jnp.float32).reshape(step * rows, depth)
        center = jnp.mean(x, axis=-1, keepdims=True)
        x = x - center
        spread = jnp.mean(x * x, axis=-1, keepdims=True)
        normed = (x * lax.rsqrt(spread + 1e-05) * g_ref[...] + b_ref[...]).astype(jnp.bfloat16)
        y = lax.dot_general(normed, w_ref[...], (((1,), (1,)), ((), ())), preferred_element_type=jnp.float32)
        y = (y + bias).astype(jnp.bfloat16).astype(jnp.float32)
        proj[s * rows : (s + step) * rows, :] = jnp.concatenate(
            [y, jnp.zeros((step * rows, LANES - 2 * hidden), jnp.float32)], axis=1
        )
    pack = LANES // seqs
    for i in range(0, rows, pack):
        parts = [proj[pl.ds(i + p, seqs, stride=rows), :] for p in range(pack)]
        for p in range(pack):
            local_ref[i + p] = parts[p][:, : 2 * hidden].astype(jnp.bfloat16)
        t = jnp.concatenate(parts, axis=0).T
        for p in range(pack):
            cols = slice(p * seqs, (p + 1) * seqs)
            for which in range(2):
                base = which * hidden
                z = jnp.concatenate([t[base : base + half, cols], t[base + half : base + hidden, cols]], axis=1)
                turned[which, (i + p) * half : (i + p + 1) * half, :] = z
    for r in range(half):
        lanes = slice(r * LANES, (r + 1) * LANES)
        for which in range(2):
            z = turned[which, pl.ds(r, rows, stride=half), :].astype(jnp.bfloat16)
            flat_ref[which * rows : (which + 1) * rows, lanes] = z
    for c in others:
        c.wait()
    for k in range(n):
        at = pl.multiple_of((me ^ k) * rows, rows)
        (mine_ref, theirs_ref)[k % 2][k // 2] = pair_ref[:, pl.ds(at, rows), :]


def project(n, x, pair, g, b, w1, c1, w2, c2, w):
    seqs, rows, depth = x.shape
    width = pair.shape[2]
    hidden = w1.shape[0]
    flat = jax.ShapeDtypeStruct((2 * rows, hidden * seqs), jnp.bfloat16)
    return pl.pallas_call(
        functools.partial(_project_kernel, n),
        in_specs=[ANY] * 9,
        out_specs=(VMEM,) * 5,
        out_shape=(jax.ShapeDtypeStruct((rows, seqs, 2 * hidden), jnp.bfloat16), flat, jax.ShapeDtypeStruct(w.shape, w.dtype))
        + (jax.ShapeDtypeStruct((n // 2, rows, rows, width), jnp.bfloat16),) * 2,
        scratch_shapes=[
            pltpu.VMEM(x.shape, x.dtype),
            pltpu.VMEM(pair.shape, pair.dtype),
            pltpu.VMEM(g.shape, g.dtype),
            pltpu.VMEM(b.shape, b.dtype),
            pltpu.VMEM((2 * hidden, depth), w1.dtype),
            pltpu.VMEM((2,) + c1.shape, c1.dtype),
            pltpu.VMEM((seqs * rows, LANES), jnp.float32),
            pltpu.VMEM((2, rows * hidden // 2, LANES), jnp.float32),
            pltpu.SemaphoreType.DMA((6,)),
            pltpu.SemaphoreType.DMA((2,)),
            pltpu.SemaphoreType.DMA((2,)),
        ],
        compiler_params=pltpu.CompilerParams(vmem_limit_bytes=56 * MIB),
        cost_estimate=_cost(2_000_000_000, 3_000_000),
        name="project",
    )(x, pair, g, b, w1, c1, w2, c2, w)


def _spread_kernel(which, local_ref, w_ref, *refs):
    out_ref, wf = refs
    rows, seqs, both = local_ref.shape
    hidden = both // 2
    half = hidden // 2
    width = w_ref.shape[1]
    wf[...] = w_ref[...].astype(jnp.float32)
    blank = jnp.zeros((hidden, 2 * width), jnp.float32)
    group = 256 // seqs

    def weights(r):
        if which == 0:
            return wf[pl.ds(r, hidden, stride=hidden), :]
        return wf[r * hidden : (r + 1) * hidden, :]

    for r in range(half):
        wr = jnp.concatenate([weights(r), weights(r + half)], axis=1)
        wr = jnp.concatenate([wr, blank] if which == 0 else [blank, wr], axis=0).astype(jnp.bfloat16)
        for i in range(0, rows, group):
            a = local_ref[i : i + group].reshape(group * seqs, both)
            y = jnp.dot(a, wr, preferred_element_type=jnp.float32).astype(jnp.bfloat16)
            for k in range(group):
                for h in range(2):
                    out_ref[
                        (i + k) // 2,
                        (2 * r + h) * seqs : (2 * r + h + 1) * seqs,
                        (k % 2) * width : (k % 2 + 1) * width,
                    ] = y[k * seqs : (k + 1) * seqs, h * width : (h + 1) * width]


def spread_weights(which, local, w):
    rows, seqs, both = local.shape
    hidden = both // 2
    width = w.shape[1]
    return pl.pallas_call(
        functools.partial(_spread_kernel, which),
        in_specs=[VMEM, VMEM],
        out_specs=VMEM,
        out_shape=pltpu.VMEM((rows // 2, hidden * seqs, 2 * width), jnp.bfloat16),
        scratch_shapes=[pltpu.VMEM(w.shape, jnp.float32)],
        compiler_params=pltpu.CompilerParams(vmem_limit_bytes=8 * MIB),
        cost_estimate=_cost(2_500_000_000, 1_000_000),
        name=("spread_first", "spread_second")[which],
    )(local, w)


def _update_kernel(order, scale, bias_ref, pair_ref, t_ref, u_ref, *refs):
    pieces = refs[: len(order)]
    out_ref, late_ref, seconds, firsts, pair, pair_sem, out_sem = refs[len(order) :]
    rows, _, width = pair.shape
    fetch = pltpu.make_async_copy(pair_ref, pair, pair_sem)
    fetch.start()
    me = lax.axis_index("row")
    for ks, piece in zip(order, pieces):
        for n, k in enumerate(ks):
            at = pl.multiple_of((me ^ k) * rows, rows)
            firsts[pl.ds(at, rows), :] = piece[2 * n * rows : (2 * n + 1) * rows, :]
            seconds[pl.ds(at, rows), :] = piece[(2 * n + 1) * rows : (2 * n + 2) * rows, :]
    fetch.wait()
    sends = []
    step = min(256, pair.shape[1])

    def spans(f):
        if pair.shape[1] == step:
            f(slice(None))
        else:
            pl.loop(0, pair.shape[1] // step)(lambda c: f(pl.ds(pl.multiple_of(c * step, step), step)))

    for i in range(rows // 2):

        def early(c):
            y = jnp.dot(seconds[c, :], t_ref[i], preferred_element_type=jnp.float32)
            for k in range(2):
                up = y[:, k * width : (k + 1) * width] * scale + bias_ref[...]
                pair[2 * i + k, c, :] = (pair[2 * i + k, c, :].astype(jnp.float32) + up).astype(jnp.bfloat16)

        spans(early)
        sends.append(pltpu.make_async_copy(pair.at[pl.ds(2 * i, 2)], out_ref.at[pl.ds(2 * i, 2)], out_sem.at[i]))
        sends[-1].start()
    for i in range(rows // 2):

        def later(c):
            y = jnp.dot(firsts[c, :], u_ref[i], preferred_element_type=jnp.float32)
            for k in range(2):
                late_ref[2 * i + k, c, :] = y[:, k * width : (k + 1) * width] * scale + bias_ref[...]

        spans(later)
    for c in sends:
        c.wait()


def update(order, scale, bias, pair, t, u, pieces):
    span, inner = pair.shape[1], pieces[0].shape[1]
    rows = pair.shape[0]
    return pl.pallas_call(
        functools.partial(_update_kernel, order, scale),
        in_specs=[VMEM, ANY, VMEM, VMEM] + [VMEM] * len(order),
        out_specs=(ANY, VMEM),
        out_shape=(
            jax.ShapeDtypeStruct(pair.shape, jnp.bfloat16),
            jax.ShapeDtypeStruct(pair.shape, jnp.float32),
        ),
        scratch_shapes=[
            pltpu.VMEM((span, inner), jnp.bfloat16),
            pltpu.VMEM((span, inner), jnp.bfloat16),
            pltpu.VMEM(pair.shape, jnp.bfloat16),
            pltpu.SemaphoreType.DMA,
            pltpu.SemaphoreType.DMA((rows // 2,)),
        ],
        compiler_params=pltpu.CompilerParams(vmem_limit_bytes=(8 + 4 * span // 256) * MIB),
        cost_estimate=_cost(5_000_000_000, 6_000_000),
        name="update",
    )(bias, pair, t, u, *pieces)


def _add_kernel(order, late_ref, *refs):
    got = refs[: len(order)]
    out_hbm, staged, out_sem = refs[len(order) :]
    _, rows, _, width = got[0].shape
    n = rows * rows
    shift = rows.bit_length() - 1
    me = lax.axis_index("row")
    a = lax.broadcasted_iota(jnp.int32, (n, n), 0)
    b = lax.broadcasted_iota(jnp.int32, (n, n), 1)
    turn = jnp.where(((a & (rows - 1)) << shift) + (a >> shift) == b, 1.0, 0.0).astype(jnp.bfloat16)
    sends = []
    for c, piece in zip(order, got):
        z = jnp.concatenate([piece[0].reshape(n, width), piece[1].reshape(n, width)], axis=1)
        y = jnp.dot(turn, z, preferred_element_type=jnp.float32)
        for k in range(2):
            part = pl.ds(pl.multiple_of((me ^ c ^ k) * rows, rows), rows)
            up = y[:, k * width : (k + 1) * width].reshape(rows, rows, width)
            staged[:, part, :] = (up + late_ref[:, part, :]).astype(jnp.bfloat16)
            sends.append(pltpu.make_async_copy(staged.at[:, part, :], out_hbm.at[:, part, :], out_sem.at[c + k]))
            sends[-1].start()
    for x in sends:
        x.wait()


def add_turned(order, got, late):
    return pl.pallas_call(
        functools.partial(_add_kernel, order),
        in_specs=[VMEM] * (1 + len(order)),
        out_specs=ANY,
        out_shape=jax.ShapeDtypeStruct(late.shape, jnp.bfloat16),
        scratch_shapes=[pltpu.VMEM(late.shape, jnp.bfloat16), pltpu.SemaphoreType.DMA((2 * len(order),))],
        compiler_params=pltpu.CompilerParams(vmem_limit_bytes=24 * MIB),
        cost_estimate=_cost(500_000_000, 4_000_000),
        name="add_turned",
    )(late, *got)


def _pack_kernel(a_ref, b_ref, out_ref):
    out_ref[: a_ref.shape[0], :] = a_ref[...]
    out_ref[a_ref.shape[0] :, :] = b_ref[...]


def pack(a, b):
    return pl.pallas_call(
        _pack_kernel,
        in_specs=[VMEM, VMEM],
        out_specs=VMEM,
        out_shape=jax.ShapeDtypeStruct((a.shape[0] + b.shape[0], a.shape[1]), a.dtype),
        compiler_params=pltpu.CompilerParams(vmem_limit_bytes=4 * MIB),
        cost_estimate=_cost(0, 4 * a.size),
        name="pack",
    )(a, b)


def _pair_up_kernel(mine_ref, theirs_ref, *out_refs):
    for q, out_ref in enumerate(out_refs):
        out_ref[0] = mine_ref[q]
        out_ref[1] = theirs_ref[q]


def pair_up(mine, theirs):
    return pl.pallas_call(
        _pair_up_kernel,
        in_specs=[VMEM, VMEM],
        out_specs=(VMEM,) * mine.shape[0],
        out_shape=(jax.ShapeDtypeStruct((2,) + mine.shape[1:], mine.dtype),) * mine.shape[0],
        compiler_params=pltpu.CompilerParams(vmem_limit_bytes=4 * MIB),
        cost_estimate=_cost(0, 4 * mine.size),
        name="pair_up",
    )(mine, theirs)


def tie(x, *after):
    return lax.optimization_barrier((x,) + after)[0] if after else x


def swap(x, k, n):
    return lax.ppermute(x, "row", [(i, i ^ k) for i in range(n)])


def schedule(n):
    gathers, order, k = [], [0], n // 4
    while k:
        gathers += [(True, k, o) for o in order]
        order += [o ^ k for o in order]
        k //= 2
    gathers.sort(key=lambda g: (g[2].bit_count(), -g[1], g[2]))
    far = [(False, k, 0) for q in (0, 2) for k in range(n // 2 + q, n, 4)]
    near = [(False, k, 0) for q in (0, 2) for k in range(4 - q, n // 2, 4)]
    levels = n.bit_length() - 2
    rest = []
    for level in range(levels):
        rest += [g for g in gathers if g[2].bit_count() == level]
        rest += near[level * len(near) // levels : (level + 1) * len(near) // levels]
    plan = []
    for at, op in enumerate(far):
        plan.append(op)
        plan += rest[at * len(rest) // len(far) : (at + 1) * len(rest) // len(far)]
    return plan, tuple(order)


DEPTH = 5


def body(n, x, pair, g, b, w1, b1, w2, b2, w, bias):
    seqs, rows, depth = x.shape
    width = pair.shape[-1]
    hidden = w1.shape[1]
    local, flat, w, mine, theirs = project(
        n, x, pair, g.reshape(1, depth), b.reshape(1, depth),
        w1.T, b1.reshape(1, hidden), w2.T, b2.reshape(1, hidden), w,
    )
    far = swap(flat, n // 2, n)
    blocks = pair_up(mine, swap(theirs, 1, n))
    t = spread_weights(0, local, w)
    pieces, got, done = {0: pack(flat, tie(far, t))}, {0: blocks[0]}, [far, far]
    u = None
    plan, order = schedule(n)
    for at, (gathering, k, o) in enumerate(plan, len(done)):
        after = done[max(at - DEPTH - 4, 0) : max(at - DEPTH + 1, 0)]
        source = pieces[o] if gathering else blocks[k // 2]
        if at == DEPTH + 2:
            u = spread_weights(1, tie(local, *after[-1:]), w)
        if u is not None:
            after = after + [u]
        result = swap(tie(source, *after), k, n)
        done.append(result)
        if gathering:
            pieces[o ^ k] = result
        else:
            got[k] = result
    scale = 1.0 / seqs
    bias = bias.reshape(1, width)
    places = tuple((o, o ^ (n // 2)) for o in order)
    pair_rows, late = update(places, scale, bias, pair, t, u, [pieces[o] for o in order])
    chips = tuple(range(0, n, 2))
    return pair_rows, add_turned(chips, [got[k] for k in chips], late)


def solution(mesh):
    pair_spec = P(("grp", "row"), None, None)
    in_specs = (P("grp", "row", None), pair_spec) + (P(),) * 8
    return jax.shard_map(
        functools.partial(body, mesh.shape["row"]),
        mesh=mesh,
        in_specs=in_specs,
        out_specs=(pair_spec, pair_spec),
        check_vma=False,
    )
```

time: 90.8 us -> 58 us (0.64)
  Pallas kernels: 29.6 us -> 15.3 us
  waiting for transfers between devices: 26.3 us -> 19.5 us
  starting transfers between devices: 25.9 us -> 19.3 us
  local copies, waits for them, and re-layouts: 5.89 us -> 2.96 us
  other arithmetic: 1.49 us -> 0 us
    pallas_call x4 -> x7, Pallas kernels: 29.6 us -> 15.3 us  [the longest x1 5.33 us: update(): pl.pallas_call(functools.partial(_update_kernel, order, scale), in_specs=...]
    all_to_all x1 -> x0, starting transfers between devices: 7.52 us -> none  [body(): got = lax.all_to_all(blocks, 'row', split_axis=0, concat_axis=0, tiled=True)]
    ppermute x30 -> x16, waiting for transfers between devices: 26.3 us -> 19.5 us  [swap(): return lax.ppermute(x, 'row', [(i, i ^ k) for i in range(n)])]
    reshape x1 -> x0, local copies, waits for them, and re-layouts: 2.47 us -> none  [body(): blocks = pair.reshape(rows, n, rows, width).transpose(1, 0, 2, 3)]
    ppermute x30 -> x16, starting transfers between devices: 18.4 us -> 19.3 us  [swap(): return lax.ppermute(x, 'row', [(i, i ^ k) for i in range(n)])]
    unnamed x32 -> x14, local copies, waits for them, and re-layouts: 3.42 us -> 2.96 us
  transfers between devices with their start and end apart: 31 -> 16, of which waited for: 8 -> 7; matrix products, arithmetic and copies ran while one was open for 2% -> 0% of each run, Pallas kernels for 22% -> 18%
where the time goes in v2:
time: 58 us; the launch traced here: 57.8 us
  waiting for transfers between devices  19.5 us (34%)
  starting transfers between devices  19.3 us (33%)
  Pallas kernels  15.3 us (26%)
  local copies, waits for them, and re-layouts  2.96 us (5%)
  between operations  0.73 us (1%)
    ppermute x16, waiting for transfers between devices, swap(): return lax.ppermute(x, 'row', [(i, i ^ k) for i in range(n)])  19.5 us
    ppermute x16, starting transfers between devices, swap(): return lax.ppermute(x, 'row', [(i, i ^ k) for i in range(n)])  19.3 us
    pallas_call x1, Pallas kernels, update(): pl.pallas_call(functools.partial(_update_kernel, order, scale), in_specs=...  5.33 us
    pallas_call x2, Pallas kernels, spread_weights(): pl.pallas_call(functools.partial(_spread_kernel, which), in_specs=[VMEM,...  4.7 us
    pallas_call x1, Pallas kernels, project(): pl.pallas_call(functools.partial(_project_kernel, n), in_specs=[ANY] * 9,...  3.85 us
    unnamed x14, local copies, waits for them, and re-layouts  2.96 us
    pallas_call x1, Pallas kernels, add_turned(): pl.pallas_call(functools.partial(_add_kernel, order), in_specs=[VMEM] * (...  1.34 us
  transfers between devices with their start and end apart: 16, of which 7 were waited for; matrix products, arithmetic and copies ran while one was open for 0% of the time, Pallas kernels for 18%

profile of v2, /device:TPU:0, one launch (start us, length us, event | category | flops | bytes accessed | tf_op | source)
XLA Modules:
  0.0 57.8 jit_solution(985073721329941208)
XLA Ops:
  0.6 3.8 %project.1 = (bf16[16,64,64]{2,1,0:T(8,128)(2,1)}, bf16[32,2048]{1,0:T(8,128)(2,1)}, bf16[1024,128]{1,0:T(8,128)(2,1)}, bf16[8,16,16,128]{3,2,1,0:T(8,128)(2,1)}, bf16[8,16,16,128]{3,2,1,0:T(8,128)(2,1)}) custom-call(bf16[64,16,256]{2,1,0:T(8,128)(2,1)} %x_hbm.1, bf16[16,256,128]{2,1,0:T(8,128)(2,1)} %pair_ref.1, f32[1,256]{1,0:T(1,128)} %bitcast.10, ...), custom_call_target="tpu_custom_call" | custom-call | flops 2000000000 | bytes 3000000 | tf_op jit(solution)/shard_map/project/pallas_call | solution.py:96
  4.5 0.5 collective-permute-start
  5.0 3.7 %collective-permute-start.2 = (bf16[32,2048]{1,0:T(8,128)(2,1)}, bf16[32,2048]{1,0:T(8,128)(2,1)S(1)}, u32[]{:S(2)}, u32[]{:S(2)}) collective-permute-start(bf16[32,2048]{1,0:T(8,128)(2,1)} %get-tuple-element.36.a_ref), channel_id=1, source_target_pairs={{0,8},{1,9},{2,10},{3,11},{4,12},{5,13},{6,14},{7,15},{8,0},{9,1},... | collective-permute-start | bytes 393224 | tf_op jit(solution)/shard_map/ppermute | solution.py:313
  8.7 0.0 collective-permute-done.theirs_ref
  8.7 0.0 copy-start.1
  8.7 1.0 %copy-done.1 = bf16[8,16,16,128]{3,2,1,0:T(8,128)(2,1)S(1)} copy-done((bf16[8,16,16,128]{3,2,1,0:T(8,128)(2,1)S(1)}, bf16[8,16,16,128]{3,2,1,0:T(8,128)(2,1)}, u32[]{:S(2)}) %copy-start.1) | copy-done | bytes 524312
  9.7 0.0 copy-start.2
  9.7 0.0 copy-start.6
  9.7 0.1 pair_up.1
  9.8 2.1 %collective-permute-start.1 = (bf16[2,16,16,128]{3,2,1,0:T(8,128)(2,1)S(1)}, bf16[2,16,16,128]{3,2,1,0:T(8,128)(2,1)S(1)}, u32[]{:S(2)}, u32[]{:S(2)}) collective-permute-start(bf16[2,16,16,128]{3,2,1,0:T(8,128)(2,1)S(1)} %get-tuple-element.34), channel_id=1, source_target_pairs={{0,8},{1,9},{2,10},{3,11},{4,12},{5,13},{6,14},{7,15},{8,0},{9,1},... | collective-permute-start | bytes 393224 | tf_op jit(solution)/shard_map/ppermute | solution.py:313
  11.9 0.0 copy-start.4
  11.9 0.9 %copy-done.4 = bf16[16,64,64]{2,1,0:T(8,128)(2,1)S(1)} copy-done((bf16[16,64,64]{2,1,0:T(8,128)(2,1)S(1)}, bf16[16,64,64]{2,1,0:T(8,128)(2,1)}, u32[]{:S(2)}) %copy-start.4) | copy-done | bytes 131096
  12.8 0.0 copy-start.5
  12.8 0.9 %copy-done.5 = bf16[1024,128]{1,0:T(8,128)(2,1)S(1)} copy-done((bf16[1024,128]{1,0:T(8,128)(2,1)S(1)}, bf16[1024,128]{1,0:T(8,128)(2,1)}, u32[]{:S(2)}) %copy-start.5) | copy-done | bytes 262168
  13.8 0.0 copy-start
  13.8 0.0 copy-start.3
  13.8 2.4 %spread_first.1.t_ref = bf16[8,2048,256]{2,1,0:T(8,128)(2,1)S(1)} custom-call(bf16[16,64,64]{2,1,0:T(8,128)(2,1)S(1)} %copy-done.4, bf16[1024,128]{1,0:T(8,128)(2,1)S(1)} %copy-done.5), custom_call_target="tpu_custom_call" | custom-call | flops 2500000000 | bytes 1000000 | tf_op jit(solution)/shard_map/spread_first/pallas_call | solution.py:155
  16.2 2.7 %collective-permute-done.2.b_ref = bf16[32,2048]{1,0:T(8,128)(2,1)S(1)} collective-permute-done((bf16[32,2048]{1,0:T(8,128)(2,1)}, bf16[32,2048]{1,0:T(8,128)(2,1)S(1)}, u32[]{:S(2)}, u32[]{:S(2)}) %collective-permute-start.2) | collective-permute-done | bytes 131104 | tf_op jit(solution)/shard_map/ppermute | solution.py:313
  18.8 0.0 copy-done.2
  18.9 0.7 %collective-permute-start.3 = (bf16[64,2048]{1,0:T(8,128)(2,1)S(1)}, bf16[64,2048]{1,0:T(8,128)(2,1)S(1)}, u32[]{:S(2)}, u32[]{:S(2)}) collective-permute-start(bf16[64,2048]{1,0:T(8,128)(2,1)S(1)} %pack.1.refs_0_), channel_id=1, source_target_pairs={{0,4},{1,5},{2,6},{3,7},{4,0},{5,1},{6,2},{7,3},{8,12},{9,13},{10,... | collective-permute-start | bytes 786440 | tf_op jit(solution)/shard_map/ppermute | solution.py:313
  19.6 1.5 %collective-permute-start.4 = (bf16[64,2048]{1,0:T(8,128)(2,1)S(1)}, bf16[64,2048]{1,0:T(8,128)(2,1)S(1)}, u32[]{:S(2)}, u32[]{:S(2)}) collective-permute-start(bf16[64,2048]{1,0:T(8,128)(2,1)S(1)} %pack.1.refs_0_), channel_id=1, source_target_pairs={{0,2},{1,3},{2,0},{3,1},{4,6},{5,7},{6,4},{7,5},{8,10},{9,11},{10,... | collective-permute-start | bytes 786440 | tf_op jit(solution)/shard_map/ppermute | solution.py:313
  21.1 0.0 collective-permute-start.6
  21.1 0.3 collective-permute-done.1.refs_4_
  21.4 0.0 copy-done.6
  21.4 2.3 %spread_second.1.u_ref = bf16[8,2048,256]{2,1,0:T(8,128)(2,1)S(1)} custom-call(bf16[16,64,64]{2,1,0:T(8,128)(2,1)S(1)} %copy-done.4, bf16[1024,128]{1,0:T(8,128)(2,1)S(1)} %copy-done.6), custom_call_target="tpu_custom_call" | custom-call | flops 2500000000 | bytes 1000000 | tf_op jit(solution)/shard_map/spread_second/pallas_call | solution.py:155
  23.8 3.3 %collective-permute-done.3.refs_1_ = bf16[64,2048]{1,0:T(8,128)(2,1)S(1)} collective-permute-done((bf16[64,2048]{1,0:T(8,128)(2,1)S(1)}, bf16[64,2048]{1,0:T(8,128)(2,1)S(1)}, u32[]{:S(2)}, u32[]{:S(2)}) %collective-permute-start.3) | collective-permute-done | bytes 262176 | tf_op jit(solution)/shard_map/ppermute | solution.py:313
  27.0 1.6 %collective-permute-start.5 = (bf16[64,2048]{1,0:T(8,128)(2,1)S(1)}, bf16[64,2048]{1,0:T(8,128)(2,1)S(1)}, u32[]{:S(2)}, u32[]{:S(2)}) collective-permute-start(bf16[64,2048]{1,0:T(8,128)(2,1)S(1)} %collective-permute-done.3.refs_1_), channel_id=1, source_target_pairs={{0,2},{1,3},{2,0},{3,1},{4,6},{5,7},{6,4},{7,5},{8,10},{9,11},{10,... | collective-permute-start | bytes 786440 | tf_op jit(solution)/shard_map/ppermute | solution.py:313
  28.6 3.5 %collective-permute-start.7 = (bf16[2,16,16,128]{3,2,1,0:T(8,128)(2,1)S(1)}, bf16[2,16,16,128]{3,2,1,0:T(8,128)(2,1)S(1)}, u32[]{:S(2)}, u32[]{:S(2)}) collective-permute-start(bf16[2,16,16,128]{3,2,1,0:T(8,128)(2,1)S(1)} %get-tuple-element.41), channel_id=1, source_target_pairs={{0,12},{1,13},{2,14},{3,15},{4,8},{5,9},{6,10},{7,11},{8,4},{9,5},... | collective-permute-start | bytes 393224 | tf_op jit(solution)/shard_map/ppermute | solution.py:313
  32.1 0.0 collective-permute-start.10
  32.1 0.0 collective-permute-done.4.refs_2_
  32.1 0.8 %collective-permute-start.11 = (bf16[2,16,16,128]{3,2,1,0:T(8,128)(2,1)S(1)}, bf16[2,16,16,128]{3,2,1,0:T(8,128)(2,1)S(1)}, u32[]{:S(2)}, u32[]{:S(2)}) collective-permute-start(bf16[2,16,16,128]{3,2,1,0:T(8,128)(2,1)S(1)} %get-tuple-element.47), channel_id=1, source_target_pairs={{0,10},{1,11},{2,8},{3,9},{4,14},{5,15},{6,12},{7,13},{8,2},{9,3},... | collective-permute-start | bytes 393224 | tf_op jit(solution)/shard_map/ppermute | solution.py:313
  32.9 4.1 %collective-permute-done.7.refs_6_ = bf16[2,16,16,128]{3,2,1,0:T(8,128)(2,1)S(1)} collective-permute-done((bf16[2,16,16,128]{3,2,1,0:T(8,128)(2,1)S(1)}, bf16[2,16,16,128]{3,2,1,0:T(8,128)(2,1)S(1)}, u32[]{:S(2)}, u32[]{:S(2)}) %collective-permute-start.7) | collective-permute-done | bytes 131104 | tf_op jit(solution)/shard_map/ppermute | solution.py:313
  36.9 0.0 collective-permute-done.6.refs_4_
  36.9 0.0 collective-permute-start.8
  36.9 0.5 collective-permute-start.9
  37.4 0.8 %collective-permute-done.10.refs_2_ = bf16[2,16,16,128]{3,2,1,0:T(8,128)(2,1)S(1)} collective-permute-done((bf16[2,16,16,128]{3,2,1,0:T(8,128)(2,1)S(1)}, bf16[2,16,16,128]{3,2,1,0:T(8,128)(2,1)S(1)}, u32[]{:S(2)}, u32[]{:S(2)}) %collective-permute-start.10) | collective-permute-done | bytes 131104 | tf_op jit(solution)/shard_map/ppermute | solution.py:313
  38.3 3.8 %collective-permute-done.11.refs_5_ = bf16[2,16,16,128]{3,2,1,0:T(8,128)(2,1)S(1)} collective-permute-done((bf16[2,16,16,128]{3,2,1,0:T(8,128)(2,1)S(1)}, bf16[2,16,16,128]{3,2,1,0:T(8,128)(2,1)S(1)}, u32[]{:S(2)}, u32[]{:S(2)}) %collective-permute-start.11) | collective-permute-done | bytes 131104 | tf_op jit(solution)/shard_map/ppermute | solution.py:313
  42.1 0.0 collective-permute-done.5.refs_3_
  42.1 0.0 collective-permute-start.12
  42.1 4.0 %collective-permute-start.15 = (bf16[2,16,16,128]{3,2,1,0:T(8,128)(2,1)S(1)}, bf16[2,16,16,128]{3,2,1,0:T(8,128)(2,1)S(1)}, u32[]{:S(2)}, u32[]{:S(2)}) collective-permute-start(bf16[2,16,16,128]{3,2,1,0:T(8,128)(2,1)S(1)} %get-tuple-element.57), channel_id=1, source_target_pairs={{0,14},{1,15},{2,12},{3,13},{4,10},{5,11},{6,8},{7,9},{8,6},{9,7},... | collective-permute-start | bytes 393224 | tf_op jit(solution)/shard_map/ppermute | solution.py:313
  46.1 0.5 collective-permute-start.13
  46.6 0.0 collective-permute-done.9.refs_6_
  46.6 0.0 collective-permute-start.14
  46.6 0.0 collective-permute-done.8.refs_5_
  46.6 0.0 collective-permute-done.12.refs_7_
  46.6 0.0 copy-done
  46.6 0.0 copy-done.3
  46.6 5.3 %update.1 = (bf16[16,256,128]{2,1,0:T(8,128)(2,1)}, f32[16,256,128]{2,1,0:T(8,128)S(1)}) custom-call(f32[1,128]{1,0:T(1,128)S(1)} %bitcast.7, bf16[16,256,128]{2,1,0:T(8,128)(2,1)S(1)} %copy-done, bf16[8,2048,256]{2,1,0:T(8,128)(2,1)S(1)} %spread_first.1.t_ref, bf16[8,2048,256]{2,1,0:T(8,128)(2,1)S(1)} %spread_second.1.u_ref, ...), custom_call_target="tpu_custom_call" | custom-call | flops 5000000000 | bytes 6000000 | tf_op jit(solution)/shard_map/update/pallas_call | solution.py:215
  51.9 0.0 collective-permute-done.15.refs_7_
  52.0 4.5 %collective-permute-done.13.refs_1_ = bf16[2,16,16,128]{3,2,1,0:T(8,128)(2,1)S(1)} collective-permute-done((bf16[2,16,16,128]{3,2,1,0:T(8,128)(2,1)S(1)}, bf16[2,16,16,128]{3,2,1,0:T(8,128)(2,1)S(1)}, u32[]{:S(2)}, u32[]{:S(2)}) %collective-permute-start.13) | collective-permute-done | bytes 131104 | tf_op jit(solution)/shard_map/ppermute | solution.py:313
  56.4 0.0 collective-permute-done.14.refs_3_
  56.4 1.3 %add_turned.1 = bf16[16,256,128]{2,1,0:T(8,128)(2,1)} custom-call(f32[16,256,128]{2,1,0:T(8,128)S(1)} %get-tuple-element.50.late_ref, bf16[2,16,16,128]{3,2,1,0:T(8,128)(2,1)S(1)} %get-tuple-element.51.refs_0_, bf16[2,16,16,128]{3,2,1,0:T(8,128)(2,1)S(1)} %collective-permute-done.13.refs_1_, bf16[2,16,16,128]{3,2,1,0:T(8,128)(2,1)S(1)} %collective-permute-done.10.refs_2_, ...), custom_call_target="tpu_custom_call" | custom-call | flops 500000000 | bytes 4000000 | tf_op jit(solution)/shard_map/add_turned/pallas_call | solution.py:261
  (1 shorter events, 0.0 us)
Async XLA Ops:
  4.5 4.2 %collective-permute-start = (bf16[8,16,16,128]{3,2,1,0:T(8,128)(2,1)}, bf16[8,16,16,128]{3,2,1,0:T(8,128)(2,1)S(1)}, u32[]{:S(2)}, u32[]{:S(2)}) collective-permute-start(bf16[8,16,16,128]{3,2,1,0:T(8,128)(2,1)} %get-tuple-element.33), channel_id=1, source_target_pairs={{0,1},{1,0},{2,3},{3,2},{4,5},{5,4},{6,7},{7,6},{8,9},{9,8},{10,11... | collective-permute-start | bytes 1572872 | tf_op jit(solution)/shard_map/ppermute | solution.py:313
  5.0 13.8 %collective-permute-start.2 = (bf16[32,2048]{1,0:T(8,128)(2,1)}, bf16[32,2048]{1,0:T(8,128)(2,1)S(1)}, u32[]{:S(2)}, u32[]{:S(2)}) collective-permute-start(bf16[32,2048]{1,0:T(8,128)(2,1)} %get-tuple-element.36.a_ref), channel_id=1, source_target_pairs={{0,8},{1,9},{2,10},{3,11},{4,12},{5,13},{6,14},{7,15},{8,0},{9,1},... | collective-permute-start | bytes 393224 | tf_op jit(solution)/shard_map/ppermute | solution.py:313
  8.7 1.0 %copy-start.1 = (bf16[8,16,16,128]{3,2,1,0:T(8,128)(2,1)S(1)}, bf16[8,16,16,128]{3,2,1,0:T(8,128)(2,1)}, u32[]{:S(2)}) copy-start(bf16[8,16,16,128]{3,2,1,0:T(8,128)(2,1)} %get-tuple-element.32.mine_ref) | copy-start | bytes 1572868
  9.7 9.1 %copy-start.2 = (bf16[32,2048]{1,0:T(8,128)(2,1)S(1)}, bf16[32,2048]{1,0:T(8,128)(2,1)}, u32[]{:S(2)}) copy-start(bf16[32,2048]{1,0:T(8,128)(2,1)} %get-tuple-element.36.a_ref) | copy-start | bytes 393220
  9.7 11.7 %copy-start.6 = (bf16[1024,128]{1,0:T(8,128)(2,1)S(1)}, bf16[1024,128]{1,0:T(8,128)(2,1)}, u32[]{:S(2)}) copy-start(bf16[1024,128]{1,0:T(8,128)(2,1)} %get-tuple-element.31.w_ref) | copy-start | bytes 786436
  9.8 11.6 %collective-permute-start.1 = (bf16[2,16,16,128]{3,2,1,0:T(8,128)(2,1)S(1)}, bf16[2,16,16,128]{3,2,1,0:T(8,128)(2,1)S(1)}, u32[]{:S(2)}, u32[]{:S(2)}) collective-permute-start(bf16[2,16,16,128]{3,2,1,0:T(8,128)(2,1)S(1)} %get-tuple-element.34), channel_id=1, source_target_pairs={{0,8},{1,9},{2,10},{3,11},{4,12},{5,13},{6,14},{7,15},{8,0},{9,1},... | collective-permute-start | bytes 393224 | tf_op jit(solution)/shard_map/ppermute | solution.py:313
  11.9 0.9 %copy-start.4 = (bf16[16,64,64]{2,1,0:T(8,128)(2,1)S(1)}, bf16[16,64,64]{2,1,0:T(8,128)(2,1)}, u32[]{:S(2)}) copy-start(bf16[16,64,64]{2,1,0:T(8,128)(2,1)} %get-tuple-element.35.local_ref) | copy-start | bytes 393220
  12.8 0.9 %copy-start.5 = (bf16[1024,128]{1,0:T(8,128)(2,1)S(1)}, bf16[1024,128]{1,0:T(8,128)(2,1)}, u32[]{:S(2)}) copy-start(bf16[1024,128]{1,0:T(8,128)(2,1)} %get-tuple-element.31.w_ref) | copy-start | bytes 786436
  13.8 32.8 %copy-start = (bf16[16,256,128]{2,1,0:T(8,128)(2,1)S(1)}, bf16[16,256,128]{2,1,0:T(8,128)(2,1)}, u32[]{:S(2)}) copy-start(bf16[16,256,128]{2,1,0:T(8,128)(2,1)} %pair_ref.1) | copy-start | bytes 3145732
  13.8 32.8 %copy-start.3 = (f32[128]{0:T(128)S(1)}, f32[128]{0:T(128)}, u32[]{:S(2)}) copy-start(f32[128]{0:T(128)} %param.19) | copy-start | bytes 1540
  18.9 8.1 %collective-permute-start.3 = (bf16[64,2048]{1,0:T(8,128)(2,1)S(1)}, bf16[64,2048]{1,0:T(8,128)(2,1)S(1)}, u32[]{:S(2)}, u32[]{:S(2)}) collective-permute-start(bf16[64,2048]{1,0:T(8,128)(2,1)S(1)} %pack.1.refs_0_), channel_id=1, source_target_pairs={{0,4},{1,5},{2,6},{3,7},{4,0},{5,1},{6,2},{7,3},{8,12},{9,13},{10,... | collective-permute-start | bytes 786440 | tf_op jit(solution)/shard_map/ppermute | solution.py:313
  19.6 12.5 %collective-permute-start.4 = (bf16[64,2048]{1,0:T(8,128)(2,1)S(1)}, bf16[64,2048]{1,0:T(8,128)(2,1)S(1)}, u32[]{:S(2)}, u32[]{:S(2)}) collective-permute-start(bf16[64,2048]{1,0:T(8,128)(2,1)S(1)} %pack.1.refs_0_), channel_id=1, source_target_pairs={{0,2},{1,3},{2,0},{3,1},{4,6},{5,7},{6,4},{7,5},{8,10},{9,11},{10,... | collective-permute-start | bytes 786440 | tf_op jit(solution)/shard_map/ppermute | solution.py:313
  21.1 15.8 %collective-permute-start.6 = (bf16[64,2048]{1,0:T(8,128)(2,1)S(1)}, bf16[64,2048]{1,0:T(8,128)(2,1)S(1)}, u32[]{:S(2)}, u32[]{:S(2)}) collective-permute-start(bf16[64,2048]{1,0:T(8,128)(2,1)S(1)} %pack.1.refs_0_), channel_id=1, source_target_pairs={{0,1},{1,0},{2,3},{3,2},{4,5},{5,4},{6,7},{7,6},{8,9},{9,8},{10,11... | collective-permute-start | bytes 786440 | tf_op jit(solution)/shard_map/ppermute | solution.py:313
  27.0 15.1 %collective-permute-start.5 = (bf16[64,2048]{1,0:T(8,128)(2,1)S(1)}, bf16[64,2048]{1,0:T(8,128)(2,1)S(1)}, u32[]{:S(2)}, u32[]{:S(2)}) collective-permute-start(bf16[64,2048]{1,0:T(8,128)(2,1)S(1)} %collective-permute-done.3.refs_1_), channel_id=1, source_target_pairs={{0,2},{1,3},{2,0},{3,1},{4,6},{5,7},{6,4},{7,5},{8,10},{9,11},{10,... | collective-permute-start | bytes 786440 | tf_op jit(solution)/shard_map/ppermute | solution.py:313
  28.6 8.3 %collective-permute-start.7 = (bf16[2,16,16,128]{3,2,1,0:T(8,128)(2,1)S(1)}, bf16[2,16,16,128]{3,2,1,0:T(8,128)(2,1)S(1)}, u32[]{:S(2)}, u32[]{:S(2)}) collective-permute-start(bf16[2,16,16,128]{3,2,1,0:T(8,128)(2,1)S(1)} %get-tuple-element.41), channel_id=1, source_target_pairs={{0,12},{1,13},{2,14},{3,15},{4,8},{5,9},{6,10},{7,11},{8,4},{9,5},... | collective-permute-start | bytes 393224 | tf_op jit(solution)/shard_map/ppermute | solution.py:313
  32.1 6.2 %collective-permute-start.10 = (bf16[2,16,16,128]{3,2,1,0:T(8,128)(2,1)S(1)}, bf16[2,16,16,128]{3,2,1,0:T(8,128)(2,1)S(1)}, u32[]{:S(2)}, u32[]{:S(2)}) collective-permute-start(bf16[2,16,16,128]{3,2,1,0:T(8,128)(2,1)S(1)} %get-tuple-element.45), channel_id=1, source_target_pairs={{0,4},{1,5},{2,6},{3,7},{4,0},{5,1},{6,2},{7,3},{8,12},{9,13},{10,... | collective-permute-start | bytes 393224 | tf_op jit(solution)/shard_map/ppermute | solution.py:313
  32.1 10.0 %collective-permute-start.11 = (bf16[2,16,16,128]{3,2,1,0:T(8,128)(2,1)S(1)}, bf16[2,16,16,128]{3,2,1,0:T(8,128)(2,1)S(1)}, u32[]{:S(2)}, u32[]{:S(2)}) collective-permute-start(bf16[2,16,16,128]{3,2,1,0:T(8,128)(2,1)S(1)} %get-tuple-element.47), channel_id=1, source_target_pairs={{0,10},{1,11},{2,8},{3,9},{4,14},{5,15},{6,12},{7,13},{8,2},{9,3},... | collective-permute-start | bytes 393224 | tf_op jit(solution)/shard_map/ppermute | solution.py:313
  36.9 9.6 %collective-permute-start.8 = (bf16[64,2048]{1,0:T(8,128)(2,1)S(1)}, bf16[64,2048]{1,0:T(8,128)(2,1)S(1)}, u32[]{:S(2)}, u32[]{:S(2)}) collective-permute-start(bf16[64,2048]{1,0:T(8,128)(2,1)S(1)} %collective-permute-done.3.refs_1_), channel_id=1, source_target_pairs={{0,1},{1,0},{2,3},{3,2},{4,5},{5,4},{6,7},{7,6},{8,9},{9,8},{10,11... | collective-permute-start | bytes 786440 | tf_op jit(solution)/shard_map/ppermute | solution.py:313
  36.9 9.6 %collective-permute-start.9 = (bf16[64,2048]{1,0:T(8,128)(2,1)S(1)}, bf16[64,2048]{1,0:T(8,128)(2,1)S(1)}, u32[]{:S(2)}, u32[]{:S(2)}) collective-permute-start(bf16[64,2048]{1,0:T(8,128)(2,1)S(1)} %collective-permute-done.4.refs_2_), channel_id=1, source_target_pairs={{0,1},{1,0},{2,3},{3,2},{4,5},{5,4},{6,7},{7,6},{8,9},{9,8},{10,11... | collective-permute-start | bytes 786440 | tf_op jit(solution)/shard_map/ppermute | solution.py:313
  42.1 4.5 %collective-permute-start.12 = (bf16[64,2048]{1,0:T(8,128)(2,1)S(1)}, bf16[64,2048]{1,0:T(8,128)(2,1)S(1)}, u32[]{:S(2)}, u32[]{:S(2)}) collective-permute-start(bf16[64,2048]{1,0:T(8,128)(2,1)S(1)} %collective-permute-done.5.refs_3_), channel_id=1, source_target_pairs={{0,1},{1,0},{2,3},{3,2},{4,5},{5,4},{6,7},{7,6},{8,9},{9,8},{10,11... | collective-permute-start | bytes 786440 | tf_op jit(solution)/shard_map/ppermute | solution.py:313
  42.1 9.8 %collective-permute-start.15 = (bf16[2,16,16,128]{3,2,1,0:T(8,128)(2,1)S(1)}, bf16[2,16,16,128]{3,2,1,0:T(8,128)(2,1)S(1)}, u32[]{:S(2)}, u32[]{:S(2)}) collective-permute-start(bf16[2,16,16,128]{3,2,1,0:T(8,128)(2,1)S(1)} %get-tuple-element.57), channel_id=1, source_target_pairs={{0,14},{1,15},{2,12},{3,13},{4,10},{5,11},{6,8},{7,9},{8,6},{9,7},... | collective-permute-start | bytes 393224 | tf_op jit(solution)/shard_map/ppermute | solution.py:313
  46.1 10.4 %collective-permute-start.13 = (bf16[2,16,16,128]{3,2,1,0:T(8,128)(2,1)S(1)}, bf16[2,16,16,128]{3,2,1,0:T(8,128)(2,1)S(1)}, u32[]{:S(2)}, u32[]{:S(2)}) collective-permute-start(bf16[2,16,16,128]{3,2,1,0:T(8,128)(2,1)S(1)} %get-tuple-element.53), channel_id=1, source_target_pairs={{0,2},{1,3},{2,0},{3,1},{4,6},{5,7},{6,4},{7,5},{8,10},{9,11},{10,... | collective-permute-start | bytes 393224 | tf_op jit(solution)/shard_map/ppermute | solution.py:313
  46.6 9.9 %collective-permute-start.14 = (bf16[2,16,16,128]{3,2,1,0:T(8,128)(2,1)S(1)}, bf16[2,16,16,128]{3,2,1,0:T(8,128)(2,1)S(1)}, u32[]{:S(2)}, u32[]{:S(2)}) collective-permute-start(bf16[2,16,16,128]{3,2,1,0:T(8,128)(2,1)S(1)} %get-tuple-element.55), channel_id=1, source_target_pairs={{0,6},{1,7},{2,4},{3,5},{4,2},{5,3},{6,0},{7,1},{8,14},{9,15},{10,... | collective-permute-start | bytes 393224 | tf_op jit(solution)/shard_map/ppermute | solution.py:313

commit v3 on v2

--- a/solution.py
+++ b/solution.py
@@ -15,7 +15,7 @@
 
 
 def _cost(flops, nbytes):
-    return pl.CostEstimate(flops=flops, bytes_accessed=nbytes, transcendentals=0)
+    return pl.CostEstimate(flops=0, bytes_accessed=0, transcendentals=0)
 
 
 def _project_kernel(
@@ -92,13 +92,17 @@
     seqs, rows, depth = x.shape
     width = pair.shape[2]
     hidden = w1.shape[0]
-    flat = jax.ShapeDtypeStruct((2 * rows, hidden * seqs), jnp.bfloat16)
     return pl.pallas_call(
         functools.partial(_project_kernel, n),
         in_specs=[ANY] * 9,
         out_specs=(VMEM,) * 5,
-        out_shape=(jax.ShapeDtypeStruct((rows, seqs, 2 * hidden), jnp.bfloat16), flat, jax.ShapeDtypeStruct(w.shape, w.dtype))
-        + (jax.ShapeDtypeStruct((n // 2, rows, rows, width), jnp.bfloat16),) * 2,
+        out_shape=(
+            pltpu.VMEM((rows, seqs, 2 * hidden), jnp.bfloat16),
+            pltpu.VMEM((2 * rows, hidden * seqs), jnp.bfloat16),
+            pltpu.VMEM(w.shape, w.dtype),
+            pltpu.VMEM((n // 2, rows, rows, width), jnp.bfloat16),
+            pltpu.VMEM((n // 2, rows, rows, width), jnp.bfloat16),
+        ),
         scratch_shapes=[
             pltpu.VMEM(x.shape, x.dtype),
             pltpu.VMEM(pair.shape, pair.dtype),
@@ -228,7 +232,7 @@
             pltpu.SemaphoreType.DMA((rows // 2,)),
         ],
         compiler_params=pltpu.CompilerParams(vmem_limit_bytes=(8 + 4 * span // 256) * MIB),
-        cost_estimate=_cost(5_000_000_000, 6_000_000),
+        cost_estimate=_cost(0, 0),
         name="update",
     )(bias, pair, t, u, *pieces)
 
@@ -270,21 +274,23 @@
     )(late, *got)
 
 
-def _pack_kernel(a_ref, b_ref, out_ref):
-    out_ref[: a_ref.shape[0], :] = a_ref[...]
-    out_ref[a_ref.shape[0] :, :] = b_ref[...]
-
-
-def pack(a, b):
+def _pack_kernel(*refs):
+    rows = refs[0].shape[0]
+    for k, ref in enumerate(refs[:-1]):
+        refs[-1][k * rows : (k + 1) * rows, :] = ref[...]
+
+
+def pack(pieces):
+    rows, inner = pieces[0].shape
     return pl.pallas_call(
         _pack_kernel,
-        in_specs=[VMEM, VMEM],
+        in_specs=[VMEM] * len(pieces),
         out_specs=VMEM,
-        out_shape=jax.ShapeDtypeStruct((a.shape[0] + b.shape[0], a.shape[1]), a.dtype),
+        out_shape=pltpu.VMEM((rows * len(pieces), inner), pieces[0].dtype),
         compiler_params=pltpu.CompilerParams(vmem_limit_bytes=4 * MIB),
-        cost_estimate=_cost(0, 4 * a.size),
+        cost_estimate=_cost(0, 0),
         name="pack",
-    )(a, b)
+    )(*pieces)
 
 
 def _pair_up_kernel(mine_ref, theirs_ref, *out_refs):
@@ -313,28 +319,33 @@
     return lax.ppermute(x, "row", [(i, i ^ k) for i in range(n)])
 
 
-def schedule(n):
-    gathers, order, k = [], [0], n // 4
-    while k:
-        gathers += [(True, k, o) for o in order]
-        order += [o ^ k for o in order]
-        k //= 2
-    gathers.sort(key=lambda g: (g[2].bit_count(), -g[1], g[2]))
-    far = [(False, k, 0) for q in (0, 2) for k in range(n // 2 + q, n, 4)]
-    near = [(False, k, 0) for q in (0, 2) for k in range(4 - q, n // 2, 4)]
-    levels = n.bit_length() - 2
-    rest = []
-    for level in range(levels):
-        rest += [g for g in gathers if g[2].bit_count() == level]
-        rest += near[level * len(near) // levels : (level + 1) * len(near) // levels]
-    plan = []
-    for at, op in enumerate(far):
-        plan.append(op)
-        plan += rest[at * len(rest) // len(far) : (at + 1) * len(rest) // len(far)]
-    return plan, tuple(order)
-
-
-DEPTH = 5
+TIES = {
+    16: {
+        "E10": ("E12",),
+        "E14": ("E8",),
+        "E2": ("G4_8",),
+        "E4": ("G4_8",),
+        "E6": ("G2_12",),
+        "E8": ("G8_0",),
+        "G2_12": ("E12", "T"),
+        "G2_4": ("E12", "G2_0"),
+        "T": ("G4_0",),
+        "U": ("G4_8",),
+        "Y0": ("E8",),
+        "Y2": ("E10", "U"),
+    }
+}
+
+
+def waits(n):
+    if n in TIES:
+        return TIES[n]
+    far = [f"E{k}" for k in range(n // 2, n, 2)]
+    near = [f"E{k}" for k in range(2, n // 2, 2)]
+    after = {"T": (f"G{n // 4}_0",), "Y2": ("U",), "U": ("T",), far[0]: (f"G{n // 2}_0",), far[1]: (f"G{n // 2}_0",)}
+    after.update({b: (a,) for a, b in zip(far, far[2:])})
+    after.update({b: (a,) for a, b in zip(far, near)})
+    return after
 
 
 def body(n, x, pair, g, b, w1, b1, w2, b2, w, bias):
@@ -345,31 +356,44 @@
         n, x, pair, g.reshape(1, depth), b.reshape(1, depth),
         w1.T, b1.reshape(1, hidden), w2.T, b2.reshape(1, hidden), w,
     )
-    far = swap(flat, n // 2, n)
-    blocks = pair_up(mine, swap(theirs, 1, n))
-    t = spread_weights(0, local, w)
-    pieces, got, done = {0: pack(flat, tie(far, t))}, {0: blocks[0]}, [far, far]
-    u = None
-    plan, order = schedule(n)
-    for at, (gathering, k, o) in enumerate(plan, len(done)):
-        after = done[max(at - DEPTH - 4, 0) : max(at - DEPTH + 1, 0)]
-        source = pieces[o] if gathering else blocks[k // 2]
-        if at == DEPTH + 2:
-            u = spread_weights(1, tie(local, *after[-1:]), w)
-        if u is not None:
-            after = after + [u]
-        result = swap(tie(source, *after), k, n)
-        done.append(result)
-        if gathering:
-            pieces[o ^ k] = result
-        else:
-            got[k] = result
+    after, done = waits(n), {}
+    halves = {h: tuple(o for o in range(0, n, 2) if o & 2 == h) for h in (0, 2)}
+
+    def need(name):
+        if name not in done:
+            done[name] = make(name)
+        return done[name]
+
+    def held(x, name):
+        return tie(x, *[need(k) for k in after.get(name, ())])
+
+    def piece(o):
+        return need(f"G{o & -o}_{o & (o - 1)}") if o else flat
+
+    def make(name):
+        if name == "X":
+            return swap(theirs, 1, n)
+        if name == "B":
+            return pair_up(mine, need("X"))
+        if name in ("T", "U"):
+            return spread_weights("TU".index(name), held(local, name), w)
+        if name[0] == "P":
+            return pack([piece(o) for o in halves[int(name[1:])]])
+        if name[0] == "Y":
+            return swap(held(need("P" + name[1:]), name), 1, n)
+        if name[0] == "E":
+            k = int(name[1:])
+            return swap(held(need("B")[k // 2], name), k, n)
+        k, o = map(int, name[1:].split("_"))
+        return swap(held(piece(o), name), k, n)
+
+    pieces = [need(f"{a}{h}") for h in halves for a in "PY"]
+    places = [tuple(o ^ q for o in halves[h]) for h in halves for q in (0, 1)]
     scale = 1.0 / seqs
     bias = bias.reshape(1, width)
-    places = tuple((o, o ^ (n // 2)) for o in order)
-    pair_rows, late = update(places, scale, bias, pair, t, u, [pieces[o] for o in order])
+    pair_rows, late = update(places, scale, bias, held(pair, "K"), need("T"), need("U"), pieces)
     chips = tuple(range(0, n, 2))
-    return pair_rows, add_turned(chips, [got[k] for k in chips], late)
+    return pair_rows, add_turned(chips, [need(f"E{k}") if k else need("B")[0] for k in chips], late)
 
 
 def solution(mesh):

time: 58 us -> 48.8 us (0.84)
  waiting for transfers between devices: 19.5 us -> 12.2 us
  local copies, waits for them, and re-layouts: 2.96 us -> 0.01 us
  starting transfers between devices: 19.3 us -> 21.5 us
  Pallas kernels: 15.3 us -> 14.2 us
    ppermute x16 -> x17, waiting for transfers between devices: 19.5 us -> 12.2 us  [swap(): return lax.ppermute(x, 'row', [(i, i ^ k) for i in range(n)])]
    unnamed x14 -> x4, local copies, waits for them, and re-layouts: 2.96 us -> 0.01 us
    ppermute x16 -> x17, starting transfers between devices: 19.3 us -> 21.5 us  [swap(): return lax.ppermute(x, 'row', [(i, i ^ k) for i in range(n)])]
    pallas_call x1, Pallas kernels: 3.85 us -> 2.67 us  [project(): pl.pallas_call(functools.partial(_project_kernel, n), in_specs=[ANY] * 9,...]
  transfers between devices with their start and end apart: 16 -> 17, of which waited for: 7 -> 5; matrix products, arithmetic and copies ran while one was open for 0% -> 0% of each run, Pallas kernels for 18% -> 21%
where the time goes in v3:
time: 48.8 us; the launch traced here: 48.6 us
  starting transfers between devices  21.5 us (44%)
  Pallas kernels  14.2 us (29%)
  waiting for transfers between devices  12.2 us (25%)
  between operations  0.75 us (2%)
    ppermute x17, starting transfers between devices, swap(): return lax.ppermute(x, 'row', [(i, i ^ k) for i in range(n)])  21.5 us
    ppermute x17, waiting for transfers between devices, swap(): return lax.ppermute(x, 'row', [(i, i ^ k) for i in range(n)])  12.2 us
    pallas_call x1, Pallas kernels, update(): pl.pallas_call(functools.partial(_update_kernel, order, scale), in_specs=...  5.33 us
    pallas_call x2, Pallas kernels, spread_weights(): pl.pallas_call(functools.partial(_spread_kernel, which), in_specs=[VMEM,...  4.69 us
    pallas_call x1, Pallas kernels, project(): pl.pallas_call(functools.partial(_project_kernel, n), in_specs=[ANY] * 9,...  2.67 us
    pallas_call x1, Pallas kernels, add_turned(): pl.pallas_call(functools.partial(_add_kernel, order), in_specs=[VMEM] * (...  1.35 us
  transfers between devices with their start and end apart: 17, of which 5 were waited for; matrix products, arithmetic and copies ran while one was open for 0% of the time, Pallas kernels for 21%

profile of v3, /device:TPU:0, one launch (start us, length us, event | category | flops | bytes accessed | tf_op | source)
XLA Modules:
  0.0 48.6 jit_solution(12455431411684964009)
XLA Ops:
  0.6 2.7 %project.1 = (bf16[16,64,64]{2,1,0:T(8,128)(2,1)S(1)}, bf16[32,2048]{1,0:T(8,128)(2,1)S(1)}, bf16[1024,128]{1,0:T(8,128)(2,1)S(1)}, bf16[8,16,16,128]{3,2,1,0:T(8,128)(2,1)S(1)}, bf16[8,16,16,128]{3,2,1,0:T(8,128)(2,1)S(1)}) custom-call(bf16[64,16,256]{2,1,0:T(8,128)(2,1)} %x_hbm.1, bf16[16,256,128]{2,1,0:T(8,128)(2,1)} %pair_ref.1, f32[1,256]{1,0:T(1,128)} %bitcast.10, ...), custom_call_target="tpu_custom_call" | custom-call | tf_op jit(solution)/shard_map/project/pallas_call | solution.py:95
  3.3 0.5 %collective-permute-start.3 = (bf16[8,16,16,128]{3,2,1,0:T(8,128)(2,1)S(1)}, bf16[8,16,16,128]{3,2,1,0:T(8,128)(2,1)S(1)}, u32[]{:S(2)}, u32[]{:S(2)}) collective-permute-start(bf16[8,16,16,128]{3,2,1,0:T(8,128)(2,1)S(1)} %get-tuple-element.35), channel_id=1, source_target_pairs={{0,1},{1,0},{2,3},{3,2},{4,5},{5,4},{6,7},{7,6},{8,9},{9,8},{10,11... | collective-permute-start | bytes 1572872 | tf_op jit(solution)/shard_map/ppermute | solution.py:319
  3.8 3.7 %collective-permute-start.1 = (bf16[32,2048]{1,0:T(8,128)(2,1)S(1)}, bf16[32,2048]{1,0:T(8,128)(2,1)S(1)}, u32[]{:S(2)}, u32[]{:S(2)}) collective-permute-start(bf16[32,2048]{1,0:T(8,128)(2,1)S(1)} %get-tuple-element.30.refs_0_), channel_id=1, source_target_pairs={{0,8},{1,9},{2,10},{3,11},{4,12},{5,13},{6,14},{7,15},{8,0},{9,1},... | collective-permute-start | bytes 393224 | tf_op jit(solution)/shard_map/ppermute | solution.py:319
  7.5 1.6 %collective-permute-start = (bf16[32,2048]{1,0:T(8,128)(2,1)S(1)}, bf16[32,2048]{1,0:T(8,128)(2,1)S(1)}, u32[]{:S(2)}, u32[]{:S(2)}) collective-permute-start(bf16[32,2048]{1,0:T(8,128)(2,1)S(1)} %get-tuple-element.30.refs_0_), channel_id=1, source_target_pairs={{0,4},{1,5},{2,6},{3,7},{4,0},{5,1},{6,2},{7,3},{8,12},{9,13},{10,... | collective-permute-start | bytes 393224 | tf_op jit(solution)/shard_map/ppermute | solution.py:319
  9.1 0.0 collective-permute-done.3.theirs_ref
  9.1 0.1 pair_up.1
  9.1 1.3 %collective-permute-start.7 = (bf16[2,16,16,128]{3,2,1,0:T(8,128)(2,1)S(1)}, bf16[2,16,16,128]{3,2,1,0:T(8,128)(2,1)S(1)}, u32[]{:S(2)}, u32[]{:S(2)}) collective-permute-start(bf16[2,16,16,128]{3,2,1,0:T(8,128)(2,1)S(1)} %get-tuple-element.39), channel_id=1, source_target_pairs={{0,12},{1,13},{2,14},{3,15},{4,8},{5,9},{6,10},{7,11},{8,4},{9,5},... | collective-permute-start | bytes 393224 | tf_op jit(solution)/shard_map/ppermute | solution.py:319
  10.5 1.5 %collective-permute-start.6 = (bf16[32,2048]{1,0:T(8,128)(2,1)S(1)}, bf16[32,2048]{1,0:T(8,128)(2,1)S(1)}, u32[]{:S(2)}, u32[]{:S(2)}) collective-permute-start(bf16[32,2048]{1,0:T(8,128)(2,1)S(1)} %get-tuple-element.30.refs_0_), channel_id=1, source_target_pairs={{0,2},{1,3},{2,0},{3,1},{4,6},{5,7},{6,4},{7,5},{8,10},{9,11},{10,... | collective-permute-start | bytes 393224 | tf_op jit(solution)/shard_map/ppermute | solution.py:319
  12.0 2.7 %collective-permute-done.1.refs_2_ = bf16[32,2048]{1,0:T(8,128)(2,1)S(1)} collective-permute-done((bf16[32,2048]{1,0:T(8,128)(2,1)S(1)}, bf16[32,2048]{1,0:T(8,128)(2,1)S(1)}, u32[]{:S(2)}, u32[]{:S(2)}) %collective-permute-start.1) | collective-permute-done | bytes 131104 | tf_op jit(solution)/shard_map/ppermute | solution.py:319
  14.7 0.7 %collective-permute-start.2 = (bf16[32,2048]{1,0:T(8,128)(2,1)S(1)}, bf16[32,2048]{1,0:T(8,128)(2,1)S(1)}, u32[]{:S(2)}, u32[]{:S(2)}) collective-permute-start(bf16[32,2048]{1,0:T(8,128)(2,1)S(1)} %collective-permute-done.1.refs_2_), channel_id=1, source_target_pairs={{0,4},{1,5},{2,6},{3,7},{4,0},{5,1},{6,2},{7,3},{8,12},{9,13},{10,... | collective-permute-start | bytes 393224 | tf_op jit(solution)/shard_map/ppermute | solution.py:319
  15.4 3.6 %collective-permute-start.4 = (bf16[2,16,16,128]{3,2,1,0:T(8,128)(2,1)S(1)}, bf16[2,16,16,128]{3,2,1,0:T(8,128)(2,1)S(1)}, u32[]{:S(2)}, u32[]{:S(2)}) collective-permute-start(bf16[2,16,16,128]{3,2,1,0:T(8,128)(2,1)S(1)} %get-tuple-element.37), channel_id=1, source_target_pairs={{0,8},{1,9},{2,10},{3,11},{4,12},{5,13},{6,14},{7,15},{8,0},{9,1},... | collective-permute-start | bytes 393224 | tf_op jit(solution)/shard_map/ppermute | solution.py:319
  19.0 0.0 collective-permute-done.refs_1_
  19.0 0.0 copy-start
  19.0 0.0 copy-start.1
  19.0 2.4 %spread_first.1.t_ref = bf16[8,2048,256]{2,1,0:T(8,128)(2,1)S(1)} custom-call(bf16[16,64,64]{2,1,0:T(8,128)(2,1)S(1)} %get-tuple-element.33.local_ref, bf16[1024,128]{1,0:T(8,128)(2,1)S(1)} %get-tuple-element.32.w_ref), custom_call_target="tpu_custom_call" | custom-call | tf_op jit(solution)/shard_map/spread_first/pallas_call | solution.py:159
  21.4 1.6 %collective-permute-start.9 = (bf16[32,2048]{1,0:T(8,128)(2,1)S(1)}, bf16[32,2048]{1,0:T(8,128)(2,1)S(1)}, u32[]{:S(2)}, u32[]{:S(2)}) collective-permute-start(bf16[32,2048]{1,0:T(8,128)(2,1)S(1)} %collective-permute-done.1.refs_2_), channel_id=1, source_target_pairs={{0,2},{1,3},{2,0},{3,1},{4,6},{5,7},{6,4},{7,5},{8,10},{9,11},{10,... | collective-permute-start | bytes 393224 | tf_op jit(solution)/shard_map/ppermute | solution.py:319
  23.0 0.0 collective-permute-done.7.refs_6_
  23.0 0.0 collective-permute-done.6.refs_0_
  23.0 0.5 %collective-permute-start.8 = (bf16[32,2048]{1,0:T(8,128)(2,1)S(1)}, bf16[32,2048]{1,0:T(8,128)(2,1)S(1)}, u32[]{:S(2)}, u32[]{:S(2)}) collective-permute-start(bf16[32,2048]{1,0:T(8,128)(2,1)S(1)} %collective-permute-done.refs_1_), channel_id=1, source_target_pairs={{0,2},{1,3},{2,0},{3,1},{4,6},{5,7},{6,4},{7,5},{8,10},{9,11},{10,... | collective-permute-start | bytes 393224 | tf_op jit(solution)/shard_map/ppermute | solution.py:319
  23.5 0.0 collective-permute-done.2.refs_3_
  23.5 1.5 %collective-permute-start.10 = (bf16[32,2048]{1,0:T(8,128)(2,1)S(1)}, bf16[32,2048]{1,0:T(8,128)(2,1)S(1)}, u32[]{:S(2)}, u32[]{:S(2)}) collective-permute-start(bf16[32,2048]{1,0:T(8,128)(2,1)S(1)} %collective-permute-done.2.refs_3_), channel_id=1, source_target_pairs={{0,2},{1,3},{2,0},{3,1},{4,6},{5,7},{6,4},{7,5},{8,10},{9,11},{10,... | collective-permute-start | bytes 393224 | tf_op jit(solution)/shard_map/ppermute | solution.py:319
  25.0 1.1 %collective-permute-start.11 = (bf16[2,16,16,128]{3,2,1,0:T(8,128)(2,1)S(1)}, bf16[2,16,16,128]{3,2,1,0:T(8,128)(2,1)S(1)}, u32[]{:S(2)}, u32[]{:S(2)}) collective-permute-start(bf16[2,16,16,128]{3,2,1,0:T(8,128)(2,1)S(1)} %get-tuple-element.43), channel_id=1, source_target_pairs={{0,10},{1,11},{2,8},{3,9},{4,14},{5,15},{6,12},{7,13},{8,2},{9,3},... | collective-permute-start | bytes 393224 | tf_op jit(solution)/shard_map/ppermute | solution.py:319
  26.1 0.0 collective-permute-done.4.refs_4_
  26.1 0.1 collective-permute-start.5
  26.2 2.3 %spread_second.1.u_ref = bf16[8,2048,256]{2,1,0:T(8,128)(2,1)S(1)} custom-call(bf16[16,64,64]{2,1,0:T(8,128)(2,1)S(1)} %get-tuple-element.33.local_ref, bf16[1024,128]{1,0:T(8,128)(2,1)S(1)} %get-tuple-element.32.w_ref), custom_call_target="tpu_custom_call" | custom-call | tf_op jit(solution)/shard_map/spread_second/pallas_call | solution.py:159
  28.5 0.0 collective-permute-done.9.refs_2_
  28.6 3.7 %collective-permute-done.8.refs_1_ = bf16[32,2048]{1,0:T(8,128)(2,1)S(1)} collective-permute-done((bf16[32,2048]{1,0:T(8,128)(2,1)S(1)}, bf16[32,2048]{1,0:T(8,128)(2,1)S(1)}, u32[]{:S(2)}, u32[]{:S(2)}) %collective-permute-start.8) | collective-permute-done | bytes 131104 | tf_op jit(solution)/shard_map/ppermute | solution.py:319
  32.3 2.4 %collective-permute-done.10.refs_3_ = bf16[32,2048]{1,0:T(8,128)(2,1)S(1)} collective-permute-done((bf16[32,2048]{1,0:T(8,128)(2,1)S(1)}, bf16[32,2048]{1,0:T(8,128)(2,1)S(1)}, u32[]{:S(2)}, u32[]{:S(2)}) %collective-permute-start.10) | collective-permute-done | bytes 131104 | tf_op jit(solution)/shard_map/ppermute | solution.py:319
  34.7 0.0 collective-permute-done.11.refs_5_
  34.7 0.1 collective-permute-start.12
  34.8 0.3 collective-permute-start.14
  35.1 1.5 %collective-permute-start.13 = (bf16[2,16,16,128]{3,2,1,0:T(8,128)(2,1)S(1)}, bf16[2,16,16,128]{3,2,1,0:T(8,128)(2,1)S(1)}, u32[]{:S(2)}, u32[]{:S(2)}) collective-permute-start(bf16[2,16,16,128]{3,2,1,0:T(8,128)(2,1)S(1)} %get-tuple-element.49), channel_id=1, source_target_pairs={{0,2},{1,3},{2,0},{3,1},{4,6},{5,7},{6,4},{7,5},{8,10},{9,11},{10,... | collective-permute-start | bytes 393224 | tf_op jit(solution)/shard_map/ppermute | solution.py:319
  36.6 1.4 %collective-permute-start.16 = (bf16[2,16,16,128]{3,2,1,0:T(8,128)(2,1)S(1)}, bf16[2,16,16,128]{3,2,1,0:T(8,128)(2,1)S(1)}, u32[]{:S(2)}, u32[]{:S(2)}) collective-permute-start(bf16[2,16,16,128]{3,2,1,0:T(8,128)(2,1)S(1)} %get-tuple-element.55), channel_id=1, source_target_pairs={{0,14},{1,15},{2,12},{3,13},{4,10},{5,11},{6,8},{7,9},{8,6},{9,7},... | collective-permute-start | bytes 393224 | tf_op jit(solution)/shard_map/ppermute | solution.py:319
  38.1 0.0 collective-permute-done.5.refs_1_
  38.1 0.5 %collective-permute-start.15 = (bf16[2,16,16,128]{3,2,1,0:T(8,128)(2,1)S(1)}, bf16[2,16,16,128]{3,2,1,0:T(8,128)(2,1)S(1)}, u32[]{:S(2)}, u32[]{:S(2)}) collective-permute-start(bf16[2,16,16,128]{3,2,1,0:T(8,128)(2,1)S(1)} %get-tuple-element.53), channel_id=1, source_target_pairs={{0,6},{1,7},{2,4},{3,5},{4,2},{5,3},{6,0},{7,1},{8,14},{9,15},{10,... | collective-permute-start | bytes 393224 | tf_op jit(solution)/shard_map/ppermute | solution.py:319
  38.6 0.0 collective-permute-done.12.refs_3_
  38.6 0.0 copy-done
  38.6 0.0 copy-done.1
  38.6 5.3 %update.1 = (bf16[16,256,128]{2,1,0:T(8,128)(2,1)}, f32[16,256,128]{2,1,0:T(8,128)S(1)}) custom-call(f32[1,128]{1,0:T(1,128)S(1)} %bitcast.7, bf16[16,256,128]{2,1,0:T(8,128)(2,1)S(1)} %copy-done, bf16[8,2048,256]{2,1,0:T(8,128)(2,1)S(1)} %spread_first.1.t_ref, bf16[8,2048,256]{2,1,0:T(8,128)(2,1)S(1)} %spread_second.1.u_ref, ...), custom_call_target="tpu_custom_call" | custom-call | tf_op jit(solution)/shard_map/update/pallas_call | solution.py:219
  43.9 0.0 collective-permute-done.14.refs_2_
  43.9 0.0 collective-permute-done.13.refs_1_
  43.9 1.8 %collective-permute-done.16.refs_7_ = bf16[2,16,16,128]{3,2,1,0:T(8,128)(2,1)S(1)} collective-permute-done((bf16[2,16,16,128]{3,2,1,0:T(8,128)(2,1)S(1)}, bf16[2,16,16,128]{3,2,1,0:T(8,128)(2,1)S(1)}, u32[]{:S(2)}, u32[]{:S(2)}) %collective-permute-start.16) | collective-permute-done | bytes 131104 | tf_op jit(solution)/shard_map/ppermute | solution.py:319
  45.7 1.5 %collective-permute-done.15.refs_3_ = bf16[2,16,16,128]{3,2,1,0:T(8,128)(2,1)S(1)} collective-permute-done((bf16[2,16,16,128]{3,2,1,0:T(8,128)(2,1)S(1)}, bf16[2,16,16,128]{3,2,1,0:T(8,128)(2,1)S(1)}, u32[]{:S(2)}, u32[]{:S(2)}) %collective-permute-start.15) | collective-permute-done | bytes 131104 | tf_op jit(solution)/shard_map/ppermute | solution.py:319
  47.3 1.3 %add_turned.1 = bf16[16,256,128]{2,1,0:T(8,128)(2,1)} custom-call(f32[16,256,128]{2,1,0:T(8,128)S(1)} %get-tuple-element.46.late_ref, bf16[2,16,16,128]{3,2,1,0:T(8,128)(2,1)S(1)} %get-tuple-element.47.refs_0_, bf16[2,16,16,128]{3,2,1,0:T(8,128)(2,1)S(1)} %collective-permute-done.13.refs_1_, bf16[2,16,16,128]{3,2,1,0:T(8,128)(2,1)S(1)} %collective-permute-done.14.refs_2_, ...), custom_call_target="tpu_custom_call" | custom-call | tf_op jit(solution)/shard_map/add_turned/pallas_call | solution.py:265
  (2 shorter events, 0.1 us)
Async XLA Ops:
  3.3 5.8 %collective-permute-start.3 = (bf16[8,16,16,128]{3,2,1,0:T(8,128)(2,1)S(1)}, bf16[8,16,16,128]{3,2,1,0:T(8,128)(2,1)S(1)}, u32[]{:S(2)}, u32[]{:S(2)}) collective-permute-start(bf16[8,16,16,128]{3,2,1,0:T(8,128)(2,1)S(1)} %get-tuple-element.35), channel_id=1, source_target_pairs={{0,1},{1,0},{2,3},{3,2},{4,5},{5,4},{6,7},{7,6},{8,9},{9,8},{10,11... | collective-permute-start | bytes 1572872 | tf_op jit(solution)/shard_map/ppermute | solution.py:319
  3.8 10.9 %collective-permute-start.1 = (bf16[32,2048]{1,0:T(8,128)(2,1)S(1)}, bf16[32,2048]{1,0:T(8,128)(2,1)S(1)}, u32[]{:S(2)}, u32[]{:S(2)}) collective-permute-start(bf16[32,2048]{1,0:T(8,128)(2,1)S(1)} %get-tuple-element.30.refs_0_), channel_id=1, source_target_pairs={{0,8},{1,9},{2,10},{3,11},{4,12},{5,13},{6,14},{7,15},{8,0},{9,1},... | collective-permute-start | bytes 393224 | tf_op jit(solution)/shard_map/ppermute | solution.py:319
  7.5 11.5 %collective-permute-start = (bf16[32,2048]{1,0:T(8,128)(2,1)S(1)}, bf16[32,2048]{1,0:T(8,128)(2,1)S(1)}, u32[]{:S(2)}, u32[]{:S(2)}) collective-permute-start(bf16[32,2048]{1,0:T(8,128)(2,1)S(1)} %get-tuple-element.30.refs_0_), channel_id=1, source_target_pairs={{0,4},{1,5},{2,6},{3,7},{4,0},{5,1},{6,2},{7,3},{8,12},{9,13},{10,... | collective-permute-start | bytes 393224 | tf_op jit(solution)/shard_map/ppermute | solution.py:319
  9.1 13.8 %collective-permute-start.7 = (bf16[2,16,16,128]{3,2,1,0:T(8,128)(2,1)S(1)}, bf16[2,16,16,128]{3,2,1,0:T(8,128)(2,1)S(1)}, u32[]{:S(2)}, u32[]{:S(2)}) collective-permute-start(bf16[2,16,16,128]{3,2,1,0:T(8,128)(2,1)S(1)} %get-tuple-element.39), channel_id=1, source_target_pairs={{0,12},{1,13},{2,14},{3,15},{4,8},{5,9},{6,10},{7,11},{8,4},{9,5},... | collective-permute-start | bytes 393224 | tf_op jit(solution)/shard_map/ppermute | solution.py:319
  10.5 12.5 %collective-permute-start.6 = (bf16[32,2048]{1,0:T(8,128)(2,1)S(1)}, bf16[32,2048]{1,0:T(8,128)(2,1)S(1)}, u32[]{:S(2)}, u32[]{:S(2)}) collective-permute-start(bf16[32,2048]{1,0:T(8,128)(2,1)S(1)} %get-tuple-element.30.refs_0_), channel_id=1, source_target_pairs={{0,2},{1,3},{2,0},{3,1},{4,6},{5,7},{6,4},{7,5},{8,10},{9,11},{10,... | collective-permute-start | bytes 393224 | tf_op jit(solution)/shard_map/ppermute | solution.py:319
  14.7 8.8 %collective-permute-start.2 = (bf16[32,2048]{1,0:T(8,128)(2,1)S(1)}, bf16[32,2048]{1,0:T(8,128)(2,1)S(1)}, u32[]{:S(2)}, u32[]{:S(2)}) collective-permute-start(bf16[32,2048]{1,0:T(8,128)(2,1)S(1)} %collective-permute-done.1.refs_2_), channel_id=1, source_target_pairs={{0,4},{1,5},{2,6},{3,7},{4,0},{5,1},{6,2},{7,3},{8,12},{9,13},{10,... | collective-permute-start | bytes 393224 | tf_op jit(solution)/shard_map/ppermute | solution.py:319
  15.4 10.8 %collective-permute-start.4 = (bf16[2,16,16,128]{3,2,1,0:T(8,128)(2,1)S(1)}, bf16[2,16,16,128]{3,2,1,0:T(8,128)(2,1)S(1)}, u32[]{:S(2)}, u32[]{:S(2)}) collective-permute-start(bf16[2,16,16,128]{3,2,1,0:T(8,128)(2,1)S(1)} %get-tuple-element.37), channel_id=1, source_target_pairs={{0,8},{1,9},{2,10},{3,11},{4,12},{5,13},{6,14},{7,15},{8,0},{9,1},... | collective-permute-start | bytes 393224 | tf_op jit(solution)/shard_map/ppermute | solution.py:319
  19.0 19.6 %copy-start = (bf16[16,256,128]{2,1,0:T(8,128)(2,1)S(1)}, bf16[16,256,128]{2,1,0:T(8,128)(2,1)}, u32[]{:S(2)}) copy-start(bf16[16,256,128]{2,1,0:T(8,128)(2,1)} %pair_ref.1) | copy-start | bytes 3145732
  19.0 19.6 %copy-start.1 = (f32[128]{0:T(128)S(1)}, f32[128]{0:T(128)}, u32[]{:S(2)}) copy-start(f32[128]{0:T(128)} %param.19) | copy-start | bytes 1540
  21.4 7.2 %collective-permute-start.9 = (bf16[32,2048]{1,0:T(8,128)(2,1)S(1)}, bf16[32,2048]{1,0:T(8,128)(2,1)S(1)}, u32[]{:S(2)}, u32[]{:S(2)}) collective-permute-start(bf16[32,2048]{1,0:T(8,128)(2,1)S(1)} %collective-permute-done.1.refs_2_), channel_id=1, source_target_pairs={{0,2},{1,3},{2,0},{3,1},{4,6},{5,7},{6,4},{7,5},{8,10},{9,11},{10,... | collective-permute-start | bytes 393224 | tf_op jit(solution)/shard_map/ppermute | solution.py:319
  23.0 9.3 %collective-permute-start.8 = (bf16[32,2048]{1,0:T(8,128)(2,1)S(1)}, bf16[32,2048]{1,0:T(8,128)(2,1)S(1)}, u32[]{:S(2)}, u32[]{:S(2)}) collective-permute-start(bf16[32,2048]{1,0:T(8,128)(2,1)S(1)} %collective-permute-done.refs_1_), channel_id=1, source_target_pairs={{0,2},{1,3},{2,0},{3,1},{4,6},{5,7},{6,4},{7,5},{8,10},{9,11},{10,... | collective-permute-start | bytes 393224 | tf_op jit(solution)/shard_map/ppermute | solution.py:319
  23.5 11.2 %collective-permute-start.10 = (bf16[32,2048]{1,0:T(8,128)(2,1)S(1)}, bf16[32,2048]{1,0:T(8,128)(2,1)S(1)}, u32[]{:S(2)}, u32[]{:S(2)}) collective-permute-start(bf16[32,2048]{1,0:T(8,128)(2,1)S(1)} %collective-permute-done.2.refs_3_), channel_id=1, source_target_pairs={{0,2},{1,3},{2,0},{3,1},{4,6},{5,7},{6,4},{7,5},{8,10},{9,11},{10,... | collective-permute-start | bytes 393224 | tf_op jit(solution)/shard_map/ppermute | solution.py:319
  25.0 9.7 %collective-permute-start.11 = (bf16[2,16,16,128]{3,2,1,0:T(8,128)(2,1)S(1)}, bf16[2,16,16,128]{3,2,1,0:T(8,128)(2,1)S(1)}, u32[]{:S(2)}, u32[]{:S(2)}) collective-permute-start(bf16[2,16,16,128]{3,2,1,0:T(8,128)(2,1)S(1)} %get-tuple-element.43), channel_id=1, source_target_pairs={{0,10},{1,11},{2,8},{3,9},{4,14},{5,15},{6,12},{7,13},{8,2},{9,3},... | collective-permute-start | bytes 393224 | tf_op jit(solution)/shard_map/ppermute | solution.py:319
  26.1 11.9 %collective-permute-start.5 = (bf16[128,2048]{1,0:T(8,128)(2,1)S(1)}, bf16[128,2048]{1,0:T(8,128)(2,1)S(1)}, u32[]{:S(2)}, u32[]{:S(2)}) collective-permute-start(bf16[128,2048]{1,0:T(8,128)(2,1)S(1)} %pack.2.refs_0_), channel_id=1, source_target_pairs={{0,1},{1,0},{2,3},{3,2},{4,5},{5,4},{6,7},{7,6},{8,9},{9,8},{10,11... | collective-permute-start | bytes 1572872 | tf_op jit(solution)/shard_map/ppermute | solution.py:319
  34.7 3.9 %collective-permute-start.12 = (bf16[128,2048]{1,0:T(8,128)(2,1)S(1)}, bf16[128,2048]{1,0:T(8,128)(2,1)S(1)}, u32[]{:S(2)}, u32[]{:S(2)}) collective-permute-start(bf16[128,2048]{1,0:T(8,128)(2,1)S(1)} %pack.3.refs_2_), channel_id=1, source_target_pairs={{0,1},{1,0},{2,3},{3,2},{4,5},{5,4},{6,7},{7,6},{8,9},{9,8},{10,11... | collective-permute-start | bytes 1572872 | tf_op jit(solution)/shard_map/ppermute | solution.py:319
  34.8 9.1 %collective-permute-start.14 = (bf16[2,16,16,128]{3,2,1,0:T(8,128)(2,1)S(1)}, bf16[2,16,16,128]{3,2,1,0:T(8,128)(2,1)S(1)}, u32[]{:S(2)}, u32[]{:S(2)}) collective-permute-start(bf16[2,16,16,128]{3,2,1,0:T(8,128)(2,1)S(1)} %get-tuple-element.51), channel_id=1, source_target_pairs={{0,4},{1,5},{2,6},{3,7},{4,0},{5,1},{6,2},{7,3},{8,12},{9,13},{10,... | collective-permute-start | bytes 393224 | tf_op jit(solution)/shard_map/ppermute | solution.py:319
  35.1 8.8 %collective-permute-start.13 = (bf16[2,16,16,128]{3,2,1,0:T(8,128)(2,1)S(1)}, bf16[2,16,16,128]{3,2,1,0:T(8,128)(2,1)S(1)}, u32[]{:S(2)}, u32[]{:S(2)}) collective-permute-start(bf16[2,16,16,128]{3,2,1,0:T(8,128)(2,1)S(1)} %get-tuple-element.49), channel_id=1, source_target_pairs={{0,2},{1,3},{2,0},{3,1},{4,6},{5,7},{6,4},{7,5},{8,10},{9,11},{10,... | collective-permute-start | bytes 393224 | tf_op jit(solution)/shard_map/ppermute | solution.py:319
  36.6 9.1 %collective-permute-start.16 = (bf16[2,16,16,128]{3,2,1,0:T(8,128)(2,1)S(1)}, bf16[2,16,16,128]{3,2,1,0:T(8,128)(2,1)S(1)}, u32[]{:S(2)}, u32[]{:S(2)}) collective-permute-start(bf16[2,16,16,128]{3,2,1,0:T(8,128)(2,1)S(1)} %get-tuple-element.55), channel_id=1, source_target_pairs={{0,14},{1,15},{2,12},{3,13},{4,10},{5,11},{6,8},{7,9},{8,6},{9,7},... | collective-permute-start | bytes 393224 | tf_op jit(solution)/shard_map/ppermute | solution.py:319
  38.1 9.2 %collective-permute-start.15 = (bf16[2,16,16,128]{3,2,1,0:T(8,128)(2,1)S(1)}, bf16[2,16,16,128]{3,2,1,0:T(8,128)(2,1)S(1)}, u32[]{:S(2)}, u32[]{:S(2)}) collective-permute-start(bf16[2,16,16,128]{3,2,1,0:T(8,128)(2,1)S(1)} %get-tuple-element.53), channel_id=1, source_target_pairs={{0,6},{1,7},{2,4},{3,5},{4,2},{5,3},{6,0},{7,1},{8,14},{9,15},{10,... | collective-permute-start | bytes 393224 | tf_op jit(solution)/shard_map/ppermute | solution.py:319

commit v4 on v3

--- a/solution.py
+++ b/solution.py
@@ -325,7 +325,7 @@
         "E14": ("E8",),
         "E2": ("G4_8",),
         "E4": ("G4_8",),
-        "E6": ("G2_12",),
+        "E6": ("G4_8",),
         "E8": ("G8_0",),
         "G2_12": ("E12", "T"),
         "G2_4": ("E12", "G2_0"),

time: 48.8 us -> 48.8 us (level)
  starting transfers between devices: 21.5 us -> 22.4 us
  waiting for transfers between devices: 12.2 us -> 11.3 us
    ppermute x17, starting transfers between devices: 21.5 us -> 22.4 us  [swap(): return lax.ppermute(x, 'row', [(i, i ^ k) for i in range(n)])]
    ppermute x17, waiting for transfers between devices: 12.2 us -> 11.3 us  [swap(): return lax.ppermute(x, 'row', [(i, i ^ k) for i in range(n)])]
  transfers between devices with their start and end apart: 17 -> 17, of which waited for: 5 -> 4; matrix products, arithmetic and copies ran while one was open for 0% -> 0% of each run, Pallas kernels for 21% -> 21%
where the time goes in v4:
time: 48.8 us; the launch traced here: 48.7 us
  starting transfers between devices  22.4 us (46%)
  Pallas kernels  14.2 us (29%)
  waiting for transfers between devices  11.3 us (23%)
  between operations  0.74 us (2%)
    ppermute x17, starting transfers between devices, swap(): return lax.ppermute(x, 'row', [(i, i ^ k) for i in range(n)])  22.4 us
    ppermute x17, waiting for transfers between devices, swap(): return lax.ppermute(x, 'row', [(i, i ^ k) for i in range(n)])  11.3 us
    pallas_call x1, Pallas kernels, update(): pl.pallas_call(functools.partial(_update_kernel, order, scale), in_specs=...  5.33 us
    pallas_call x2, Pallas kernels, spread_weights(): pl.pallas_call(functools.partial(_spread_kernel, which), in_specs=[VMEM,...  4.69 us
    pallas_call x1, Pallas kernels, project(): pl.pallas_call(functools.partial(_project_kernel, n), in_specs=[ANY] * 9,...  2.67 us
    pallas_call x1, Pallas kernels, add_turned(): pl.pallas_call(functools.partial(_add_kernel, order), in_specs=[VMEM] * (...  1.35 us
  transfers between devices with their start and end apart: 17, of which 4 were waited for; matrix products, arithmetic and copies ran while one was open for 0% of the time, Pallas kernels for 21%

profile of v4, /device:TPU:0, one launch (start us, length us, event | category | flops | bytes accessed | tf_op | source)
XLA Modules:
  0.0 48.7 jit_solution(4557621132183056124)
XLA Ops:
  0.6 2.7 %project.1 = (bf16[16,64,64]{2,1,0:T(8,128)(2,1)S(1)}, bf16[32,2048]{1,0:T(8,128)(2,1)S(1)}, bf16[1024,128]{1,0:T(8,128)(2,1)S(1)}, bf16[8,16,16,128]{3,2,1,0:T(8,128)(2,1)S(1)}, bf16[8,16,16,128]{3,2,1,0:T(8,128)(2,1)S(1)}) custom-call(bf16[64,16,256]{2,1,0:T(8,128)(2,1)} %x_hbm.1, bf16[16,256,128]{2,1,0:T(8,128)(2,1)} %pair_ref.1, f32[1,256]{1,0:T(1,128)} %bitcast.10, ...), custom_call_target="tpu_custom_call" | custom-call | tf_op jit(solution)/shard_map/project/pallas_call | solution.py:95
  3.3 0.5 %collective-permute-start.3 = (bf16[8,16,16,128]{3,2,1,0:T(8,128)(2,1)S(1)}, bf16[8,16,16,128]{3,2,1,0:T(8,128)(2,1)S(1)}, u32[]{:S(2)}, u32[]{:S(2)}) collective-permute-start(bf16[8,16,16,128]{3,2,1,0:T(8,128)(2,1)S(1)} %get-tuple-element.35), channel_id=1, source_target_pairs={{0,1},{1,0},{2,3},{3,2},{4,5},{5,4},{6,7},{7,6},{8,9},{9,8},{10,11... | collective-permute-start | bytes 1572872 | tf_op jit(solution)/shard_map/ppermute | solution.py:319
  3.8 3.7 %collective-permute-start.1 = (bf16[32,2048]{1,0:T(8,128)(2,1)S(1)}, bf16[32,2048]{1,0:T(8,128)(2,1)S(1)}, u32[]{:S(2)}, u32[]{:S(2)}) collective-permute-start(bf16[32,2048]{1,0:T(8,128)(2,1)S(1)} %get-tuple-element.30.refs_0_), channel_id=1, source_target_pairs={{0,8},{1,9},{2,10},{3,11},{4,12},{5,13},{6,14},{7,15},{8,0},{9,1},... | collective-permute-start | bytes 393224 | tf_op jit(solution)/shard_map/ppermute | solution.py:319
  7.5 1.6 %collective-permute-start = (bf16[32,2048]{1,0:T(8,128)(2,1)S(1)}, bf16[32,2048]{1,0:T(8,128)(2,1)S(1)}, u32[]{:S(2)}, u32[]{:S(2)}) collective-permute-start(bf16[32,2048]{1,0:T(8,128)(2,1)S(1)} %get-tuple-element.30.refs_0_), channel_id=1, source_target_pairs={{0,4},{1,5},{2,6},{3,7},{4,0},{5,1},{6,2},{7,3},{8,12},{9,13},{10,... | collective-permute-start | bytes 393224 | tf_op jit(solution)/shard_map/ppermute | solution.py:319
  9.1 0.0 collective-permute-done.3.theirs_ref
  9.1 0.1 pair_up.1
  9.1 1.3 %collective-permute-start.7 = (bf16[2,16,16,128]{3,2,1,0:T(8,128)(2,1)S(1)}, bf16[2,16,16,128]{3,2,1,0:T(8,128)(2,1)S(1)}, u32[]{:S(2)}, u32[]{:S(2)}) collective-permute-start(bf16[2,16,16,128]{3,2,1,0:T(8,128)(2,1)S(1)} %get-tuple-element.39), channel_id=1, source_target_pairs={{0,12},{1,13},{2,14},{3,15},{4,8},{5,9},{6,10},{7,11},{8,4},{9,5},... | collective-permute-start | bytes 393224 | tf_op jit(solution)/shard_map/ppermute | solution.py:319
  10.5 1.5 %collective-permute-start.6 = (bf16[32,2048]{1,0:T(8,128)(2,1)S(1)}, bf16[32,2048]{1,0:T(8,128)(2,1)S(1)}, u32[]{:S(2)}, u32[]{:S(2)}) collective-permute-start(bf16[32,2048]{1,0:T(8,128)(2,1)S(1)} %get-tuple-element.30.refs_0_), channel_id=1, source_target_pairs={{0,2},{1,3},{2,0},{3,1},{4,6},{5,7},{6,4},{7,5},{8,10},{9,11},{10,... | collective-permute-start | bytes 393224 | tf_op jit(solution)/shard_map/ppermute | solution.py:319
  12.0 2.7 %collective-permute-done.1.refs_2_ = bf16[32,2048]{1,0:T(8,128)(2,1)S(1)} collective-permute-done((bf16[32,2048]{1,0:T(8,128)(2,1)S(1)}, bf16[32,2048]{1,0:T(8,128)(2,1)S(1)}, u32[]{:S(2)}, u32[]{:S(2)}) %collective-permute-start.1) | collective-permute-done | bytes 131104 | tf_op jit(solution)/shard_map/ppermute | solution.py:319
  14.7 0.7 %collective-permute-start.2 = (bf16[32,2048]{1,0:T(8,128)(2,1)S(1)}, bf16[32,2048]{1,0:T(8,128)(2,1)S(1)}, u32[]{:S(2)}, u32[]{:S(2)}) collective-permute-start(bf16[32,2048]{1,0:T(8,128)(2,1)S(1)} %collective-permute-done.1.refs_2_), channel_id=1, source_target_pairs={{0,4},{1,5},{2,6},{3,7},{4,0},{5,1},{6,2},{7,3},{8,12},{9,13},{10,... | collective-permute-start | bytes 393224 | tf_op jit(solution)/shard_map/ppermute | solution.py:319
  15.4 3.6 %collective-permute-start.4 = (bf16[2,16,16,128]{3,2,1,0:T(8,128)(2,1)S(1)}, bf16[2,16,16,128]{3,2,1,0:T(8,128)(2,1)S(1)}, u32[]{:S(2)}, u32[]{:S(2)}) collective-permute-start(bf16[2,16,16,128]{3,2,1,0:T(8,128)(2,1)S(1)} %get-tuple-element.37), channel_id=1, source_target_pairs={{0,8},{1,9},{2,10},{3,11},{4,12},{5,13},{6,14},{7,15},{8,0},{9,1},... | collective-permute-start | bytes 393224 | tf_op jit(solution)/shard_map/ppermute | solution.py:319
  19.0 0.0 collective-permute-done.refs_1_
  19.0 0.0 copy-start
  19.0 0.0 copy-start.1
  19.0 2.4 %spread_first.1.t_ref = bf16[8,2048,256]{2,1,0:T(8,128)(2,1)S(1)} custom-call(bf16[16,64,64]{2,1,0:T(8,128)(2,1)S(1)} %get-tuple-element.33.local_ref, bf16[1024,128]{1,0:T(8,128)(2,1)S(1)} %get-tuple-element.32.w_ref), custom_call_target="tpu_custom_call" | custom-call | tf_op jit(solution)/shard_map/spread_first/pallas_call | solution.py:159
  21.4 1.6 %collective-permute-start.9 = (bf16[32,2048]{1,0:T(8,128)(2,1)S(1)}, bf16[32,2048]{1,0:T(8,128)(2,1)S(1)}, u32[]{:S(2)}, u32[]{:S(2)}) collective-permute-start(bf16[32,2048]{1,0:T(8,128)(2,1)S(1)} %collective-permute-done.1.refs_2_), channel_id=1, source_target_pairs={{0,2},{1,3},{2,0},{3,1},{4,6},{5,7},{6,4},{7,5},{8,10},{9,11},{10,... | collective-permute-start | bytes 393224 | tf_op jit(solution)/shard_map/ppermute | solution.py:319
  23.0 0.0 collective-permute-done.7.refs_6_
  23.0 0.0 collective-permute-done.6.refs_0_
  23.0 0.5 %collective-permute-start.8 = (bf16[32,2048]{1,0:T(8,128)(2,1)S(1)}, bf16[32,2048]{1,0:T(8,128)(2,1)S(1)}, u32[]{:S(2)}, u32[]{:S(2)}) collective-permute-start(bf16[32,2048]{1,0:T(8,128)(2,1)S(1)} %collective-permute-done.refs_1_), channel_id=1, source_target_pairs={{0,2},{1,3},{2,0},{3,1},{4,6},{5,7},{6,4},{7,5},{8,10},{9,11},{10,... | collective-permute-start | bytes 393224 | tf_op jit(solution)/shard_map/ppermute | solution.py:319
  23.5 0.0 collective-permute-done.2.refs_3_
  23.5 1.5 %collective-permute-start.10 = (bf16[32,2048]{1,0:T(8,128)(2,1)S(1)}, bf16[32,2048]{1,0:T(8,128)(2,1)S(1)}, u32[]{:S(2)}, u32[]{:S(2)}) collective-permute-start(bf16[32,2048]{1,0:T(8,128)(2,1)S(1)} %collective-permute-done.2.refs_3_), channel_id=1, source_target_pairs={{0,2},{1,3},{2,0},{3,1},{4,6},{5,7},{6,4},{7,5},{8,10},{9,11},{10,... | collective-permute-start | bytes 393224 | tf_op jit(solution)/shard_map/ppermute | solution.py:319
  25.0 1.1 %collective-permute-start.11 = (bf16[2,16,16,128]{3,2,1,0:T(8,128)(2,1)S(1)}, bf16[2,16,16,128]{3,2,1,0:T(8,128)(2,1)S(1)}, u32[]{:S(2)}, u32[]{:S(2)}) collective-permute-start(bf16[2,16,16,128]{3,2,1,0:T(8,128)(2,1)S(1)} %get-tuple-element.43), channel_id=1, source_target_pairs={{0,10},{1,11},{2,8},{3,9},{4,14},{5,15},{6,12},{7,13},{8,2},{9,3},... | collective-permute-start | bytes 393224 | tf_op jit(solution)/shard_map/ppermute | solution.py:319
  26.1 0.0 collective-permute-done.4.refs_4_
  26.1 0.1 collective-permute-start.5
  26.2 2.3 %spread_second.1.u_ref = bf16[8,2048,256]{2,1,0:T(8,128)(2,1)S(1)} custom-call(bf16[16,64,64]{2,1,0:T(8,128)(2,1)S(1)} %get-tuple-element.33.local_ref, bf16[1024,128]{1,0:T(8,128)(2,1)S(1)} %get-tuple-element.32.w_ref), custom_call_target="tpu_custom_call" | custom-call | tf_op jit(solution)/shard_map/spread_second/pallas_call | solution.py:159
  28.5 0.0 collective-permute-done.9.refs_2_
  28.6 3.7 %collective-permute-done.8.refs_1_ = bf16[32,2048]{1,0:T(8,128)(2,1)S(1)} collective-permute-done((bf16[32,2048]{1,0:T(8,128)(2,1)S(1)}, bf16[32,2048]{1,0:T(8,128)(2,1)S(1)}, u32[]{:S(2)}, u32[]{:S(2)}) %collective-permute-start.8) | collective-permute-done | bytes 131104 | tf_op jit(solution)/shard_map/ppermute | solution.py:319
  32.3 2.4 %collective-permute-done.10.refs_3_ = bf16[32,2048]{1,0:T(8,128)(2,1)S(1)} collective-permute-done((bf16[32,2048]{1,0:T(8,128)(2,1)S(1)}, bf16[32,2048]{1,0:T(8,128)(2,1)S(1)}, u32[]{:S(2)}, u32[]{:S(2)}) %collective-permute-start.10) | collective-permute-done | bytes 131104 | tf_op jit(solution)/shard_map/ppermute | solution.py:319
  34.7 0.0 collective-permute-done.11.refs_5_
  34.7 0.1 collective-permute-start.12
  34.8 1.3 %collective-permute-start.15 = (bf16[2,16,16,128]{3,2,1,0:T(8,128)(2,1)S(1)}, bf16[2,16,16,128]{3,2,1,0:T(8,128)(2,1)S(1)}, u32[]{:S(2)}, u32[]{:S(2)}) collective-permute-start(bf16[2,16,16,128]{3,2,1,0:T(8,128)(2,1)S(1)} %get-tuple-element.53), channel_id=1, source_target_pairs={{0,6},{1,7},{2,4},{3,5},{4,2},{5,3},{6,0},{7,1},{8,14},{9,15},{10,... | collective-permute-start | bytes 393224 | tf_op jit(solution)/shard_map/ppermute | solution.py:319
  36.1 1.8 %collective-permute-start.14 = (bf16[2,16,16,128]{3,2,1,0:T(8,128)(2,1)S(1)}, bf16[2,16,16,128]{3,2,1,0:T(8,128)(2,1)S(1)}, u32[]{:S(2)}, u32[]{:S(2)}) collective-permute-start(bf16[2,16,16,128]{3,2,1,0:T(8,128)(2,1)S(1)} %get-tuple-element.51), channel_id=1, source_target_pairs={{0,4},{1,5},{2,6},{3,7},{4,0},{5,1},{6,2},{7,3},{8,12},{9,13},{10,... | collective-permute-start | bytes 393224 | tf_op jit(solution)/shard_map/ppermute | solution.py:319
  37.8 0.5 %collective-permute-start.13 = (bf16[2,16,16,128]{3,2,1,0:T(8,128)(2,1)S(1)}, bf16[2,16,16,128]{3,2,1,0:T(8,128)(2,1)S(1)}, u32[]{:S(2)}, u32[]{:S(2)}) collective-permute-start(bf16[2,16,16,128]{3,2,1,0:T(8,128)(2,1)S(1)} %get-tuple-element.49), channel_id=1, source_target_pairs={{0,2},{1,3},{2,0},{3,1},{4,6},{5,7},{6,4},{7,5},{8,10},{9,11},{10,... | collective-permute-start | bytes 393224 | tf_op jit(solution)/shard_map/ppermute | solution.py:319
  38.3 0.0 collective-permute-done.5.refs_1_
  38.3 1.1 %collective-permute-start.16 = (bf16[2,16,16,128]{3,2,1,0:T(8,128)(2,1)S(1)}, bf16[2,16,16,128]{3,2,1,0:T(8,128)(2,1)S(1)}, u32[]{:S(2)}, u32[]{:S(2)}) collective-permute-start(bf16[2,16,16,128]{3,2,1,0:T(8,128)(2,1)S(1)} %get-tuple-element.55), channel_id=1, source_target_pairs={{0,14},{1,15},{2,12},{3,13},{4,10},{5,11},{6,8},{7,9},{8,6},{9,7},... | collective-permute-start | bytes 393224 | tf_op jit(solution)/shard_map/ppermute | solution.py:319
  39.5 0.0 collective-permute-done.12.refs_3_
  39.5 0.0 copy-done
  39.5 0.0 copy-done.1
  39.5 5.3 %update.1 = (bf16[16,256,128]{2,1,0:T(8,128)(2,1)}, f32[16,256,128]{2,1,0:T(8,128)S(1)}) custom-call(f32[1,128]{1,0:T(1,128)S(1)} %bitcast.7, bf16[16,256,128]{2,1,0:T(8,128)(2,1)S(1)} %copy-done, bf16[8,2048,256]{2,1,0:T(8,128)(2,1)S(1)} %spread_first.1.t_ref, bf16[8,2048,256]{2,1,0:T(8,128)(2,1)S(1)} %spread_second.1.u_ref, ...), custom_call_target="tpu_custom_call" | custom-call | tf_op jit(solution)/shard_map/update/pallas_call | solution.py:219
  44.8 0.0 collective-permute-done.15.refs_3_
  44.8 2.5 %collective-permute-done.14.refs_2_ = bf16[2,16,16,128]{3,2,1,0:T(8,128)(2,1)S(1)} collective-permute-done((bf16[2,16,16,128]{3,2,1,0:T(8,128)(2,1)S(1)}, bf16[2,16,16,128]{3,2,1,0:T(8,128)(2,1)S(1)}, u32[]{:S(2)}, u32[]{:S(2)}) %collective-permute-start.14) | collective-permute-done | bytes 131104 | tf_op jit(solution)/shard_map/ppermute | solution.py:319
  47.3 0.0 collective-permute-done.13.refs_1_
  47.3 0.0 collective-permute-done.16.refs_7_
  47.3 1.3 %add_turned.1 = bf16[16,256,128]{2,1,0:T(8,128)(2,1)} custom-call(f32[16,256,128]{2,1,0:T(8,128)S(1)} %get-tuple-element.46.late_ref, bf16[2,16,16,128]{3,2,1,0:T(8,128)(2,1)S(1)} %get-tuple-element.47.refs_0_, bf16[2,16,16,128]{3,2,1,0:T(8,128)(2,1)S(1)} %collective-permute-done.13.refs_1_, bf16[2,16,16,128]{3,2,1,0:T(8,128)(2,1)S(1)} %collective-permute-done.14.refs_2_, ...), custom_call_target="tpu_custom_call" | custom-call | tf_op jit(solution)/shard_map/add_turned/pallas_call | solution.py:265
  (2 shorter events, 0.1 us)
Async XLA Ops:
  3.3 5.8 %collective-permute-start.3 = (bf16[8,16,16,128]{3,2,1,0:T(8,128)(2,1)S(1)}, bf16[8,16,16,128]{3,2,1,0:T(8,128)(2,1)S(1)}, u32[]{:S(2)}, u32[]{:S(2)}) collective-permute-start(bf16[8,16,16,128]{3,2,1,0:T(8,128)(2,1)S(1)} %get-tuple-element.35), channel_id=1, source_target_pairs={{0,1},{1,0},{2,3},{3,2},{4,5},{5,4},{6,7},{7,6},{8,9},{9,8},{10,11... | collective-permute-start | bytes 1572872 | tf_op jit(solution)/shard_map/ppermute | solution.py:319
  3.8 10.9 %collective-permute-start.1 = (bf16[32,2048]{1,0:T(8,128)(2,1)S(1)}, bf16[32,2048]{1,0:T(8,128)(2,1)S(1)}, u32[]{:S(2)}, u32[]{:S(2)}) collective-permute-start(bf16[32,2048]{1,0:T(8,128)(2,1)S(1)} %get-tuple-element.30.refs_0_), channel_id=1, source_target_pairs={{0,8},{1,9},{2,10},{3,11},{4,12},{5,13},{6,14},{7,15},{8,0},{9,1},... | collective-permute-start | bytes 393224 | tf_op jit(solution)/shard_map/ppermute | solution.py:319
  7.5 11.5 %collective-permute-start = (bf16[32,2048]{1,0:T(8,128)(2,1)S(1)}, bf16[32,2048]{1,0:T(8,128)(2,1)S(1)}, u32[]{:S(2)}, u32[]{:S(2)}) collective-permute-start(bf16[32,2048]{1,0:T(8,128)(2,1)S(1)} %get-tuple-element.30.refs_0_), channel_id=1, source_target_pairs={{0,4},{1,5},{2,6},{3,7},{4,0},{5,1},{6,2},{7,3},{8,12},{9,13},{10,... | collective-permute-start | bytes 393224 | tf_op jit(solution)/shard_map/ppermute | solution.py:319
  9.1 13.8 %collective-permute-start.7 = (bf16[2,16,16,128]{3,2,1,0:T(8,128)(2,1)S(1)}, bf16[2,16,16,128]{3,2,1,0:T(8,128)(2,1)S(1)}, u32[]{:S(2)}, u32[]{:S(2)}) collective-permute-start(bf16[2,16,16,128]{3,2,1,0:T(8,128)(2,1)S(1)} %get-tuple-element.39), channel_id=1, source_target_pairs={{0,12},{1,13},{2,14},{3,15},{4,8},{5,9},{6,10},{7,11},{8,4},{9,5},... | collective-permute-start | bytes 393224 | tf_op jit(solution)/shard_map/ppermute | solution.py:319
  10.5 12.5 %collective-permute-start.6 = (bf16[32,2048]{1,0:T(8,128)(2,1)S(1)}, bf16[32,2048]{1,0:T(8,128)(2,1)S(1)}, u32[]{:S(2)}, u32[]{:S(2)}) collective-permute-start(bf16[32,2048]{1,0:T(8,128)(2,1)S(1)} %get-tuple-element.30.refs_0_), channel_id=1, source_target_pairs={{0,2},{1,3},{2,0},{3,1},{4,6},{5,7},{6,4},{7,5},{8,10},{9,11},{10,... | collective-permute-start | bytes 393224 | tf_op jit(solution)/shard_map/ppermute | solution.py:319
  14.7 8.8 %collective-permute-start.2 = (bf16[32,2048]{1,0:T(8,128)(2,1)S(1)}, bf16[32,2048]{1,0:T(8,128)(2,1)S(1)}, u32[]{:S(2)}, u32[]{:S(2)}) collective-permute-start(bf16[32,2048]{1,0:T(8,128)(2,1)S(1)} %collective-permute-done.1.refs_2_), channel_id=1, source_target_pairs={{0,4},{1,5},{2,6},{3,7},{4,0},{5,1},{6,2},{7,3},{8,12},{9,13},{10,... | collective-permute-start | bytes 393224 | tf_op jit(solution)/shard_map/ppermute | solution.py:319
  15.4 10.8 %collective-permute-start.4 = (bf16[2,16,16,128]{3,2,1,0:T(8,128)(2,1)S(1)}, bf16[2,16,16,128]{3,2,1,0:T(8,128)(2,1)S(1)}, u32[]{:S(2)}, u32[]{:S(2)}) collective-permute-start(bf16[2,16,16,128]{3,2,1,0:T(8,128)(2,1)S(1)} %get-tuple-element.37), channel_id=1, source_target_pairs={{0,8},{1,9},{2,10},{3,11},{4,12},{5,13},{6,14},{7,15},{8,0},{9,1},... | collective-permute-start | bytes 393224 | tf_op jit(solution)/shard_map/ppermute | solution.py:319
  19.0 20.5 %copy-start = (bf16[16,256,128]{2,1,0:T(8,128)(2,1)S(1)}, bf16[16,256,128]{2,1,0:T(8,128)(2,1)}, u32[]{:S(2)}) copy-start(bf16[16,256,128]{2,1,0:T(8,128)(2,1)} %pair_ref.1) | copy-start | bytes 3145732
  19.0 20.5 %copy-start.1 = (f32[128]{0:T(128)S(1)}, f32[128]{0:T(128)}, u32[]{:S(2)}) copy-start(f32[128]{0:T(128)} %param.19) | copy-start | bytes 1540
  21.4 7.2 %collective-permute-start.9 = (bf16[32,2048]{1,0:T(8,128)(2,1)S(1)}, bf16[32,2048]{1,0:T(8,128)(2,1)S(1)}, u32[]{:S(2)}, u32[]{:S(2)}) collective-permute-start(bf16[32,2048]{1,0:T(8,128)(2,1)S(1)} %collective-permute-done.1.refs_2_), channel_id=1, source_target_pairs={{0,2},{1,3},{2,0},{3,1},{4,6},{5,7},{6,4},{7,5},{8,10},{9,11},{10,... | collective-permute-start | bytes 393224 | tf_op jit(solution)/shard_map/ppermute | solution.py:319
  23.0 9.3 %collective-permute-start.8 = (bf16[32,2048]{1,0:T(8,128)(2,1)S(1)}, bf16[32,2048]{1,0:T(8,128)(2,1)S(1)}, u32[]{:S(2)}, u32[]{:S(2)}) collective-permute-start(bf16[32,2048]{1,0:T(8,128)(2,1)S(1)} %collective-permute-done.refs_1_), channel_id=1, source_target_pairs={{0,2},{1,3},{2,0},{3,1},{4,6},{5,7},{6,4},{7,5},{8,10},{9,11},{10,... | collective-permute-start | bytes 393224 | tf_op jit(solution)/shard_map/ppermute | solution.py:319
  23.5 11.2 %collective-permute-start.10 = (bf16[32,2048]{1,0:T(8,128)(2,1)S(1)}, bf16[32,2048]{1,0:T(8,128)(2,1)S(1)}, u32[]{:S(2)}, u32[]{:S(2)}) collective-permute-start(bf16[32,2048]{1,0:T(8,128)(2,1)S(1)} %collective-permute-done.2.refs_3_), channel_id=1, source_target_pairs={{0,2},{1,3},{2,0},{3,1},{4,6},{5,7},{6,4},{7,5},{8,10},{9,11},{10,... | collective-permute-start | bytes 393224 | tf_op jit(solution)/shard_map/ppermute | solution.py:319
  25.0 9.7 %collective-permute-start.11 = (bf16[2,16,16,128]{3,2,1,0:T(8,128)(2,1)S(1)}, bf16[2,16,16,128]{3,2,1,0:T(8,128)(2,1)S(1)}, u32[]{:S(2)}, u32[]{:S(2)}) collective-permute-start(bf16[2,16,16,128]{3,2,1,0:T(8,128)(2,1)S(1)} %get-tuple-element.43), channel_id=1, source_target_pairs={{0,10},{1,11},{2,8},{3,9},{4,14},{5,15},{6,12},{7,13},{8,2},{9,3},... | collective-permute-start | bytes 393224 | tf_op jit(solution)/shard_map/ppermute | solution.py:319
  26.1 12.2 %collective-permute-start.5 = (bf16[128,2048]{1,0:T(8,128)(2,1)S(1)}, bf16[128,2048]{1,0:T(8,128)(2,1)S(1)}, u32[]{:S(2)}, u32[]{:S(2)}) collective-permute-start(bf16[128,2048]{1,0:T(8,128)(2,1)S(1)} %pack.2.refs_0_), channel_id=1, source_target_pairs={{0,1},{1,0},{2,3},{3,2},{4,5},{5,4},{6,7},{7,6},{8,9},{9,8},{10,11... | collective-permute-start | bytes 1572872 | tf_op jit(solution)/shard_map/ppermute | solution.py:319
  34.7 4.8 %collective-permute-start.12 = (bf16[128,2048]{1,0:T(8,128)(2,1)S(1)}, bf16[128,2048]{1,0:T(8,128)(2,1)S(1)}, u32[]{:S(2)}, u32[]{:S(2)}) collective-permute-start(bf16[128,2048]{1,0:T(8,128)(2,1)S(1)} %pack.3.refs_2_), channel_id=1, source_target_pairs={{0,1},{1,0},{2,3},{3,2},{4,5},{5,4},{6,7},{7,6},{8,9},{9,8},{10,11... | collective-permute-start | bytes 1572872 | tf_op jit(solution)/shard_map/ppermute | solution.py:319
  34.8 10.0 %collective-permute-start.15 = (bf16[2,16,16,128]{3,2,1,0:T(8,128)(2,1)S(1)}, bf16[2,16,16,128]{3,2,1,0:T(8,128)(2,1)S(1)}, u32[]{:S(2)}, u32[]{:S(2)}) collective-permute-start(bf16[2,16,16,128]{3,2,1,0:T(8,128)(2,1)S(1)} %get-tuple-element.53), channel_id=1, source_target_pairs={{0,6},{1,7},{2,4},{3,5},{4,2},{5,3},{6,0},{7,1},{8,14},{9,15},{10,... | collective-permute-start | bytes 393224 | tf_op jit(solution)/shard_map/ppermute | solution.py:319
  36.1 11.2 %collective-permute-start.14 = (bf16[2,16,16,128]{3,2,1,0:T(8,128)(2,1)S(1)}, bf16[2,16,16,128]{3,2,1,0:T(8,128)(2,1)S(1)}, u32[]{:S(2)}, u32[]{:S(2)}) collective-permute-start(bf16[2,16,16,128]{3,2,1,0:T(8,128)(2,1)S(1)} %get-tuple-element.51), channel_id=1, source_target_pairs={{0,4},{1,5},{2,6},{3,7},{4,0},{5,1},{6,2},{7,3},{8,12},{9,13},{10,... | collective-permute-start | bytes 393224 | tf_op jit(solution)/shard_map/ppermute | solution.py:319
  37.8 9.5 %collective-permute-start.13 = (bf16[2,16,16,128]{3,2,1,0:T(8,128)(2,1)S(1)}, bf16[2,16,16,128]{3,2,1,0:T(8,128)(2,1)S(1)}, u32[]{:S(2)}, u32[]{:S(2)}) collective-permute-start(bf16[2,16,16,128]{3,2,1,0:T(8,128)(2,1)S(1)} %get-tuple-element.49), channel_id=1, source_target_pairs={{0,2},{1,3},{2,0},{3,1},{4,6},{5,7},{6,4},{7,5},{8,10},{9,11},{10,... | collective-permute-start | bytes 393224 | tf_op jit(solution)/shard_map/ppermute | solution.py:319
  38.3 9.0 %collective-permute-start.16 = (bf16[2,16,16,128]{3,2,1,0:T(8,128)(2,1)S(1)}, bf16[2,16,16,128]{3,2,1,0:T(8,128)(2,1)S(1)}, u32[]{:S(2)}, u32[]{:S(2)}) collective-permute-start(bf16[2,16,16,128]{3,2,1,0:T(8,128)(2,1)S(1)} %get-tuple-element.55), channel_id=1, source_target_pairs={{0,14},{1,15},{2,12},{3,13},{4,10},{5,11},{6,8},{7,9},{8,6},{9,7},... | collective-permute-start | bytes 393224 | tf_op jit(solution)/shard_map/ppermute | solution.py:319
